TPU v7x, 32 devices: a whole 2x2x4 slice. The times are simulated.
32 devices in a mesh: lon: 8 (over z, core), lat: 4 (over y, x).
Axes of the slice: x: 2, y: 2, z: 4, core: 2. Of those that a mesh axis runs over, the one named last changes fastest.
Arguments:
- state: float32 [16, 128, 2048], P(None, 'lat', 'lon'), may hold values from -6 to 6
- coef_lon: float32 [128, 2048], P('lat', 'lon'), may hold values from 0.2 to 0.24
- coef_lat: float32 [128, 2048], P('lat', 'lon'), may hold values from 0.2 to 0.24
- land_sea: int32 [128, 2048], P('lat', 'lon'), may hold values 0 or 1
- send_cols: int32 [4, 32768], P('lat', 'lon'), may hold values from 0 to 8191
- send_count: int32 [4, 64], P('lat', 'lon'), may hold values from 64 to 512, as said below
- obs_value: float32 [16, 4, 32768], P(None, 'lat', 'lon'), may hold values from -6 to 6
- obs_weight: float32 [16, 4, 32768], P(None, 'lat', 'lon'), may hold values from 0.25 to 4
Outputs:
- increment: float32 [16, 128, 2048], P(None, 'lat', 'lon')
Inputs may be any that keep to these rules, and one draw needn't show every extreme that they name: `send_count`: at most 512 live slots go from one device to one peer; in every latitude band some receiving device gets 512 from every device of the band, which one drawn from the seed. `send_cols`: entries index a column of the sending device's own block, row-major over its 32 x 256 cells.
All inputs are finite; a program needn't handle non-finite values. No bound on the sum of `land_sea` on one device may be relied on, other than what follows from the above.
Results may differ from a plain program's by a relative error of at most 0.00002.
Values sent between devices are 32-bit elements; how exact they have to be, the bound alone decides.
A program may use at most 64 MiB of HBM per device.

v0:
```python
import jax
import jax.numpy as jnp
from jax import lax
from jax.sharding import PartitionSpec as P

PASSES = 8


def with_halo(block, sides, width):
    for axis, dim in sides:
        count = lax.axis_size(axis)
        forward = [(i, i + 1) for i in range(count - 1)]
        forward.append((count - 1, 0))
        backward = [(target, source) for source, target in forward]
        low = lax.ppermute(
            lax.slice_in_dim(block, block.shape[dim] - width, None, axis=dim), axis, forward
        )
        high = lax.ppermute(lax.slice_in_dim(block, 0, width, axis=dim), axis, backward)
        block = jnp.concatenate([low, block, high], axis=dim)
    return block


def one_pass(layer_field, east_face, north_face):
    flux_east = east_face * (layer_field[:, :, 1:] - layer_field[:, :, :-1])
    flux_north = north_face * (layer_field[:, 1:, :] - layer_field[:, :-1, :])
    return (
        layer_field[:, 1:-1, 1:-1]
        + flux_east[:, 1:-1, 1:]
        - flux_east[:, 1:-1, :-1]
        + flux_north[:, 1:, 1:-1]
        - flux_north[:, :-1, 1:-1]
    )


def body(state, coef_lon, coef_lat, land_sea, send_cols, send_count, obs_value, obs_weight):
    levels, rows_here, cols_here = state.shape
    lon_count = lax.axis_size("lon")
    lat_count = lax.axis_size("lat")
    slots = send_cols.shape[1]
    capacity = slots // lon_count
    columns = state.reshape(levels, rows_here * cols_here)
    targets = send_cols[0]
    slot_index = jnp.arange(slots, dtype=jnp.int32)
    limits = jnp.broadcast_to(send_count[0][:, None], (lon_count, capacity)).reshape(slots)
    usable = jnp.where(slot_index % capacity < limits, 1.0, 0.0).astype(jnp.float32)
    at_column = jnp.take(columns, targets, axis=1)
    remote = lax.all_to_all(at_column, "lon", split_axis=1, concat_axis=1, tiled=True)
    local_terms = obs_weight[:, 0, :] * (obs_value[:, 0, :] - remote)
    weighted = lax.all_to_all(local_terms, "lon", split_axis=1, concat_axis=1, tiled=True) * usable
    sea = land_sea.astype(jnp.float32)
    gradient = jnp.zeros((levels, rows_here * cols_here), jnp.float32).at[:, targets].add(weighted)
    gradient = gradient.reshape(levels, rows_here, cols_here) * sea[None]
    rim_width = 1
    stacked = jnp.stack([sea, coef_lon, coef_lat])
    padded = with_halo(stacked, (("lon", 2), ("lat", 1)), rim_width)
    lat_index = lax.axis_index("lat")
    row_place = jnp.arange(rows_here + 2 * rim_width, dtype=jnp.int32)
    outside = (row_place < rim_width) & (lat_index == 0) | (row_place >= rows_here + rim_width) & (
        lat_index == lat_count - 1
    )
    inside = jnp.where(outside, 0.0, 1.0).astype(jnp.float32)[:, None]
    sea_rim = padded[0] * inside
    east_face = padded[1][:, :-1] * sea_rim[:, :-1] * sea_rim[:, 1:]
    north_face = padded[2][:-1, :] * sea_rim[:-1, :] * sea_rim[1:, :]
    for step_number in range(PASSES):
        bordered = with_halo(gradient, (("lon", 2), ("lat", 1)), 1)
        gradient = one_pass(bordered, east_face, north_face)
    return gradient


def solution(mesh):
    placed = (
        P(None, "lat", "lon"),
        P("lat", "lon"),
        P("lat", "lon"),
        P("lat", "lon"),
        P("lat", "lon"),
        P("lat", "lon"),
        P(None, "lat", "lon"),
        P(None, "lat", "lon"),
    )
    return jax.shard_map(
        body, mesh=mesh, in_specs=placed, out_specs=P(None, "lat", "lon"), check_vma=False
    )
```

profile of v0, /device:TPU:0, one launch (start us, length us, event | category | flops | bytes accessed | tf_op | source)
XLA Modules:
  0.0 213.2 jit_solution(4464899643794142152)
XLA Ops:
  0.8 3.6 %copy.20 = f32[16,32,256]{0,2,1:T(8,128)} copy(f32[16,32,256]{2,1,0:T(8,128)} %param.8) | data formatting | bytes 1048576 | tf_op args[0]
  4.4 13.0 %gather_fusion = f32[4096,16]{1,0:T(8,128)S(1)} fusion(f32[16,8192]{0,1:T(8,128)} %bitcast.40, s32[4096]{0:T(1024)S(1)} %broadcast_clamp_fusion), kind=kCustom, calls=%fused_computation | custom fusion | bytes 540672 | tf_op jit(solution)/shard_map/jit(_take)/gather | solution.py:46
  20.0 6.3 %all-to-all-start = ((f32[16,8,512]{2,0,1:T(8,128)}), f32[16,8,512]{2,0,1:T(8,128)S(1)}, u32[]{:S(2)}, u32[]{:S(2)}) async-start(f32[16,8,512]{2,0,1:T(8,128)} %broadcast_select_fusion), calls=%async_computation | async-start | bytes 524288 | tf_op jit(solution)/shard_map/all_to_all | solution.py:47
  26.9 3.1 %collective-permute-start.1 = (f32[3,32,1]{2,1,0:T(8,128)S(1)}, f32[3,32,1]{2,1,0:T(8,128)S(1)}, u32[]{:S(2)}, u32[]{:S(2)}) collective-permute-start(f32[3,32,1]{2,1,0:T(8,128)S(1)} %get-tuple-element.40), channel_id=1, source_target_pairs={{4,0},{8,4},{12,8},{16,12},{20,16},{24,20},{28,24},{0,28},{5,1},{9... | collective-permute-start | bytes 1160 | tf_op jit(solution)/shard_map/ppermute | solution.py:18
  31.8 4.8 %all-to-all-done = f32[16,8,512]{2,0,1:T(8,128)S(1)} async-done(((f32[16,8,512]{2,0,1:T(8,128)}), f32[16,8,512]{2,0,1:T(8,128)S(1)}, u32[]{:S(2)}, u32[]{:S(2)}) %all-to-all-start) | async-done | bytes 262176 | tf_op jit(solution)/shard_map/all_to_all | solution.py:47
  37.6 3.4 %all-to-all-start.1 = ((f32[16,8,512]{2,0,1:T(8,128)}), f32[16,8,512]{2,0,1:T(8,128)S(1)}, u32[]{:S(2)}, u32[]{:S(2)}) async-start(f32[16,8,512]{2,0,1:T(8,128)} %copy.23), calls=%async_computation.1 | async-start | bytes 524288 | tf_op jit(solution)/shard_map/all_to_all | solution.py:49
  46.5 4.2 %all-to-all-done.1 = f32[16,8,512]{2,0,1:T(8,128)S(1)} async-done(((f32[16,8,512]{2,0,1:T(8,128)}), f32[16,8,512]{2,0,1:T(8,128)S(1)}, u32[]{:S(2)}, u32[]{:S(2)}) %all-to-all-start.1) | async-done | bytes 262176 | tf_op jit(solution)/shard_map/all_to_all | solution.py:49
  51.4 24.6 %scatter_custom_fusion = f32[16,8192]{0,1:T(8,128)} fusion(s32[4096]{0:T(1024)S(1)} %bitcast.57, f32[4096,16]{1,0:T(8,128)S(1)} %copy.25, f32[]{:T(128)} %constant.19.clone.1), kind=kCustom, calls=%fused_computation.2 | custom fusion | flops 65536 | bytes 524292 | tf_op jit(solution)/shard_map/scatter-add | solution.py:51
  75.9 2.9 %copy.26 = f32[16,32,256]{2,1,0:T(8,128)S(1)} copy(f32[16,32,256]{0,2,1:T(8,128)} %bitcast.39) | data formatting | bytes 1048576 | tf_op jit(solution)/shard_map/reshape | solution.py:52
  79.1 3.5 %collective-permute-start.5 = (f32[16,32,1]{2,1,0:T(8,128)S(1)}, f32[16,32,1]{2,1,0:T(8,128)S(1)}, u32[]{:S(2)}, u32[]{:S(2)}) collective-permute-start(f32[16,32,1]{2,1,0:T(8,128)S(1)} %get-tuple-element.36), channel_id=1, source_target_pairs={{4,0},{8,4},{12,8},{16,12},{20,16},{24,20},{28,24},{0,28},{5,1},{9... | collective-permute-start | bytes 6152 | tf_op jit(solution)/shard_map/ppermute | solution.py:18
  82.7 6.5 %collective-permute-done.4 = f32[16,32,1]{2,1,0:T(8,128)S(1)} collective-permute-done((f32[16,32,1]{2,1,0:T(8,128)S(1)}, f32[16,32,1]{2,1,0:T(8,128)S(1)}, u32[]{:S(2)}, u32[]{:S(2)}) %collective-permute-start.4) | collective-permute-done | bytes 2080 | tf_op jit(solution)/shard_map/ppermute | solution.py:15
  97.0 3.5 %collective-permute-start.9 = (f32[16,32,1]{2,1,0:T(8,128)S(1)}, f32[16,32,1]{2,1,0:T(8,128)S(1)}, u32[]{:S(2)}, u32[]{:S(2)}) collective-permute-start(f32[16,32,1]{2,1,0:T(8,128)S(1)} %get-tuple-element.34), channel_id=1, source_target_pairs={{4,0},{8,4},{12,8},{16,12},{20,16},{24,20},{28,24},{0,28},{5,1},{9... | collective-permute-start | bytes 6152 | tf_op jit(solution)/shard_map/ppermute | solution.py:18
  100.5 4.6 %collective-permute-done.8 = f32[16,32,1]{2,1,0:T(8,128)S(1)} collective-permute-done((f32[16,32,1]{2,1,0:T(8,128)S(1)}, f32[16,32,1]{2,1,0:T(8,128)S(1)}, u32[]{:S(2)}, u32[]{:S(2)}) %collective-permute-start.8) | collective-permute-done | bytes 2080 | tf_op jit(solution)/shard_map/ppermute | solution.py:15
  105.3 2.4 %collective-permute-start.10 = (f32[16,1,258]{2,1,0:T(1,128)S(1)}, f32[16,1,258]{2,1,0:T(1,128)S(1)}, u32[]{:S(2)}, u32[]{:S(2)}) collective-permute-start(f32[16,1,258]{2,1,0:T(1,128)S(1)} %get-tuple-element.17), channel_id=1, source_target_pairs={{0,1},{1,2},{2,3},{3,0},{4,5},{5,6},{6,7},{7,4},{8,9},{9,10},{10,1... | collective-permute-start | bytes 49544 | tf_op jit(solution)/shard_map/ppermute | solution.py:15
  113.8 3.5 %collective-permute-start.13 = (f32[16,32,1]{2,1,0:T(8,128)S(1)}, f32[16,32,1]{2,1,0:T(8,128)S(1)}, u32[]{:S(2)}, u32[]{:S(2)}) collective-permute-start(f32[16,32,1]{2,1,0:T(8,128)S(1)} %get-tuple-element.32), channel_id=1, source_target_pairs={{4,0},{8,4},{12,8},{16,12},{20,16},{24,20},{28,24},{0,28},{5,1},{9... | collective-permute-start | bytes 6152 | tf_op jit(solution)/shard_map/ppermute | solution.py:18
  117.3 5.5 %collective-permute-done.12 = f32[16,32,1]{2,1,0:T(8,128)S(1)} collective-permute-done((f32[16,32,1]{2,1,0:T(8,128)S(1)}, f32[16,32,1]{2,1,0:T(8,128)S(1)}, u32[]{:S(2)}, u32[]{:S(2)}) %collective-permute-start.12) | collective-permute-done | bytes 2080 | tf_op jit(solution)/shard_map/ppermute | solution.py:15
  126.0 1.8 collective-permute-done.14
  130.6 3.5 %collective-permute-start.17 = (f32[16,32,1]{2,1,0:T(8,128)S(1)}, f32[16,32,1]{2,1,0:T(8,128)S(1)}, u32[]{:S(2)}, u32[]{:S(2)}) collective-permute-start(f32[16,32,1]{2,1,0:T(8,128)S(1)} %get-tuple-element.30), channel_id=1, source_target_pairs={{4,0},{8,4},{12,8},{16,12},{20,16},{24,20},{28,24},{0,28},{5,1},{9... | collective-permute-start | bytes 6152 | tf_op jit(solution)/shard_map/ppermute | solution.py:18
  134.1 4.6 %collective-permute-done.16 = f32[16,32,1]{2,1,0:T(8,128)S(1)} collective-permute-done((f32[16,32,1]{2,1,0:T(8,128)S(1)}, f32[16,32,1]{2,1,0:T(8,128)S(1)}, u32[]{:S(2)}, u32[]{:S(2)}) %collective-permute-start.16) | collective-permute-done | bytes 2080 | tf_op jit(solution)/shard_map/ppermute | solution.py:15
  141.9 1.8 collective-permute-done.18
  146.4 3.5 %collective-permute-start.21 = (f32[16,32,1]{2,1,0:T(8,128)S(1)}, f32[16,32,1]{2,1,0:T(8,128)S(1)}, u32[]{:S(2)}, u32[]{:S(2)}) collective-permute-start(f32[16,32,1]{2,1,0:T(8,128)S(1)} %get-tuple-element.28), channel_id=1, source_target_pairs={{4,0},{8,4},{12,8},{16,12},{20,16},{24,20},{28,24},{0,28},{5,1},{9... | collective-permute-start | bytes 6152 | tf_op jit(solution)/shard_map/ppermute | solution.py:18
  149.9 5.5 %collective-permute-done.20 = f32[16,32,1]{2,1,0:T(8,128)S(1)} collective-permute-done((f32[16,32,1]{2,1,0:T(8,128)S(1)}, f32[16,32,1]{2,1,0:T(8,128)S(1)}, u32[]{:S(2)}, u32[]{:S(2)}) %collective-permute-start.20) | collective-permute-done | bytes 2080 | tf_op jit(solution)/shard_map/ppermute | solution.py:15
  158.6 1.8 collective-permute-done.22
  163.2 3.5 %collective-permute-start.25 = (f32[16,32,1]{2,1,0:T(8,128)S(1)}, f32[16,32,1]{2,1,0:T(8,128)S(1)}, u32[]{:S(2)}, u32[]{:S(2)}) collective-permute-start(f32[16,32,1]{2,1,0:T(8,128)S(1)} %get-tuple-element.26), channel_id=1, source_target_pairs={{4,0},{8,4},{12,8},{16,12},{20,16},{24,20},{28,24},{0,28},{5,1},{9... | collective-permute-start | bytes 6152 | tf_op jit(solution)/shard_map/ppermute | solution.py:18
  166.7 4.6 %collective-permute-done.24 = f32[16,32,1]{2,1,0:T(8,128)S(1)} collective-permute-done((f32[16,32,1]{2,1,0:T(8,128)S(1)}, f32[16,32,1]{2,1,0:T(8,128)S(1)}, u32[]{:S(2)}, u32[]{:S(2)}) %collective-permute-start.24) | collective-permute-done | bytes 2080 | tf_op jit(solution)/shard_map/ppermute | solution.py:15
  171.6 2.4 %collective-permute-start.26 = (f32[16,1,258]{2,1,0:T(1,128)S(1)}, f32[16,1,258]{2,1,0:T(1,128)S(1)}, u32[]{:S(2)}, u32[]{:S(2)}) collective-permute-start(f32[16,1,258]{2,1,0:T(1,128)S(1)} %get-tuple-element.9), channel_id=1, source_target_pairs={{0,1},{1,2},{2,3},{3,0},{4,5},{5,6},{6,7},{7,4},{8,9},{9,10},{10,1... | collective-permute-start | bytes 49544 | tf_op jit(solution)/shard_map/ppermute | solution.py:15
  180.0 3.5 %collective-permute-start.29 = (f32[16,32,1]{2,1,0:T(8,128)S(1)}, f32[16,32,1]{2,1,0:T(8,128)S(1)}, u32[]{:S(2)}, u32[]{:S(2)}) collective-permute-start(f32[16,32,1]{2,1,0:T(8,128)S(1)} %get-tuple-element.24), channel_id=1, source_target_pairs={{4,0},{8,4},{12,8},{16,12},{20,16},{24,20},{28,24},{0,28},{5,1},{9... | collective-permute-start | bytes 6152 | tf_op jit(solution)/shard_map/ppermute | solution.py:18
  183.6 5.5 %collective-permute-done.28 = f32[16,32,1]{2,1,0:T(8,128)S(1)} collective-permute-done((f32[16,32,1]{2,1,0:T(8,128)S(1)}, f32[16,32,1]{2,1,0:T(8,128)S(1)}, u32[]{:S(2)}, u32[]{:S(2)}) %collective-permute-start.28) | collective-permute-done | bytes 2080 | tf_op jit(solution)/shard_map/ppermute | solution.py:15
  192.3 1.8 collective-permute-done.30
  196.8 3.5 %collective-permute-start.33 = (f32[16,32,1]{2,1,0:T(8,128)S(1)}, f32[16,32,1]{2,1,0:T(8,128)S(1)}, u32[]{:S(2)}, u32[]{:S(2)}) collective-permute-start(f32[16,32,1]{2,1,0:T(8,128)S(1)} %get-tuple-element.22), channel_id=1, source_target_pairs={{4,0},{8,4},{12,8},{16,12},{20,16},{24,20},{28,24},{0,28},{5,1},{9... | collective-permute-start | bytes 6152 | tf_op jit(solution)/shard_map/ppermute | solution.py:18
  200.4 4.6 %collective-permute-done.32 = f32[16,32,1]{2,1,0:T(8,128)S(1)} collective-permute-done((f32[16,32,1]{2,1,0:T(8,128)S(1)}, f32[16,32,1]{2,1,0:T(8,128)S(1)}, u32[]{:S(2)}, u32[]{:S(2)}) %collective-permute-start.32) | collective-permute-done | bytes 2080 | tf_op jit(solution)/shard_map/ppermute | solution.py:15
  208.2 1.8 collective-permute-done.34
  (140 shorter events, 63.0 us)
Async XLA Ops:
  20.0 16.6 %all-to-all-start = ((f32[16,8,512]{2,0,1:T(8,128)}), f32[16,8,512]{2,0,1:T(8,128)S(1)}, u32[]{:S(2)}, u32[]{:S(2)}) async-start(f32[16,8,512]{2,0,1:T(8,128)} %broadcast_select_fusion), calls=%async_computation | async-start | bytes 524288 | tf_op jit(solution)/shard_map/all_to_all | solution.py:47
  26.4 14.6 %collective-permute-start = (f32[3,32,1]{2,1,0:T(8,128)S(1)}, f32[3,32,1]{2,1,0:T(8,128)S(1)}, u32[]{:S(2)}, u32[]{:S(2)}) collective-permute-start(f32[3,32,1]{2,1,0:T(8,128)S(1)} %get-tuple-element.39), channel_id=1, source_target_pairs={{0,4},{4,8},{8,12},{12,16},{16,20},{20,24},{24,28},{28,0},{1,5},{5... | collective-permute-start | bytes 1160 | tf_op jit(solution)/shard_map/ppermute | solution.py:15
  26.9 14.1 %collective-permute-start.1 = (f32[3,32,1]{2,1,0:T(8,128)S(1)}, f32[3,32,1]{2,1,0:T(8,128)S(1)}, u32[]{:S(2)}, u32[]{:S(2)}) collective-permute-start(f32[3,32,1]{2,1,0:T(8,128)S(1)} %get-tuple-element.40), channel_id=1, source_target_pairs={{4,0},{8,4},{12,8},{16,12},{20,16},{24,20},{28,24},{0,28},{5,1},{9... | collective-permute-start | bytes 1160 | tf_op jit(solution)/shard_map/ppermute | solution.py:18
  37.6 13.1 %all-to-all-start.1 = ((f32[16,8,512]{2,0,1:T(8,128)}), f32[16,8,512]{2,0,1:T(8,128)S(1)}, u32[]{:S(2)}, u32[]{:S(2)}) async-start(f32[16,8,512]{2,0,1:T(8,128)} %copy.23), calls=%async_computation.1 | async-start | bytes 524288 | tf_op jit(solution)/shard_map/all_to_all | solution.py:49
  41.2 4.6 %collective-permute-start.2 = (f32[3,1,258]{2,1,0:T(1,128)S(1)}, f32[3,1,258]{2,1,0:T(1,128)S(1)}, u32[]{:S(2)}, u32[]{:S(2)}) collective-permute-start(f32[3,1,258]{2,1,0:T(1,128)S(1)} %get-tuple-element.37), channel_id=1, source_target_pairs={{0,1},{1,2},{2,3},{3,0},{4,5},{5,6},{6,7},{7,4},{8,9},{9,10},{10,1... | collective-permute-start | bytes 9296 | tf_op jit(solution)/shard_map/ppermute | solution.py:15
  79.0 10.2 %collective-permute-start.4 = (f32[16,32,1]{2,1,0:T(8,128)S(1)}, f32[16,32,1]{2,1,0:T(8,128)S(1)}, u32[]{:S(2)}, u32[]{:S(2)}) collective-permute-start(f32[16,32,1]{2,1,0:T(8,128)S(1)} %get-tuple-element.35), channel_id=1, source_target_pairs={{0,4},{4,8},{8,12},{12,16},{16,20},{20,24},{24,28},{28,0},{1,5},{5... | collective-permute-start | bytes 6152 | tf_op jit(solution)/shard_map/ppermute | solution.py:15
  79.1 10.1 %collective-permute-start.5 = (f32[16,32,1]{2,1,0:T(8,128)S(1)}, f32[16,32,1]{2,1,0:T(8,128)S(1)}, u32[]{:S(2)}, u32[]{:S(2)}) collective-permute-start(f32[16,32,1]{2,1,0:T(8,128)S(1)} %get-tuple-element.36), channel_id=1, source_target_pairs={{4,0},{8,4},{12,8},{16,12},{20,16},{24,20},{28,24},{0,28},{5,1},{9... | collective-permute-start | bytes 6152 | tf_op jit(solution)/shard_map/ppermute | solution.py:18
  89.4 4.8 %collective-permute-start.6 = (f32[16,1,258]{2,1,0:T(1,128)S(1)}, f32[16,1,258]{2,1,0:T(1,128)S(1)}, u32[]{:S(2)}, u32[]{:S(2)}) collective-permute-start(f32[16,1,258]{2,1,0:T(1,128)S(1)} %get-tuple-element.19), channel_id=1, source_target_pairs={{0,1},{1,2},{2,3},{3,0},{4,5},{5,6},{6,7},{7,4},{8,9},{9,10},{10,1... | collective-permute-start | bytes 49544 | tf_op jit(solution)/shard_map/ppermute | solution.py:15
  96.9 8.2 %collective-permute-start.8 = (f32[16,32,1]{2,1,0:T(8,128)S(1)}, f32[16,32,1]{2,1,0:T(8,128)S(1)}, u32[]{:S(2)}, u32[]{:S(2)}) collective-permute-start(f32[16,32,1]{2,1,0:T(8,128)S(1)} %get-tuple-element.33), channel_id=1, source_target_pairs={{0,4},{4,8},{8,12},{12,16},{16,20},{20,24},{24,28},{28,0},{1,5},{5... | collective-permute-start | bytes 6152 | tf_op jit(solution)/shard_map/ppermute | solution.py:15
  97.0 8.2 %collective-permute-start.9 = (f32[16,32,1]{2,1,0:T(8,128)S(1)}, f32[16,32,1]{2,1,0:T(8,128)S(1)}, u32[]{:S(2)}, u32[]{:S(2)}) collective-permute-start(f32[16,32,1]{2,1,0:T(8,128)S(1)} %get-tuple-element.34), channel_id=1, source_target_pairs={{4,0},{8,4},{12,8},{16,12},{20,16},{24,20},{28,24},{0,28},{5,1},{9... | collective-permute-start | bytes 6152 | tf_op jit(solution)/shard_map/ppermute | solution.py:18
  105.3 4.8 %collective-permute-start.10 = (f32[16,1,258]{2,1,0:T(1,128)S(1)}, f32[16,1,258]{2,1,0:T(1,128)S(1)}, u32[]{:S(2)}, u32[]{:S(2)}) collective-permute-start(f32[16,1,258]{2,1,0:T(1,128)S(1)} %get-tuple-element.17), channel_id=1, source_target_pairs={{0,1},{1,2},{2,3},{3,0},{4,5},{5,6},{6,7},{7,4},{8,9},{9,10},{10,1... | collective-permute-start | bytes 49544 | tf_op jit(solution)/shard_map/ppermute | solution.py:15
  107.8 3.8 %collective-permute-start.11 = (f32[16,1,258]{2,1,0:T(1,128)S(1)}, f32[16,1,258]{2,1,0:T(1,128)S(1)}, u32[]{:S(2)}, u32[]{:S(2)}) collective-permute-start(f32[16,1,258]{2,1,0:T(1,128)S(1)} %get-tuple-element.18), channel_id=1, source_target_pairs={{1,0},{2,1},{3,2},{0,3},{5,4},{6,5},{7,6},{4,7},{9,8},{10,9},{11,1... | collective-permute-start | bytes 49544 | tf_op jit(solution)/shard_map/ppermute | solution.py:18
  113.7 9.1 %collective-permute-start.12 = (f32[16,32,1]{2,1,0:T(8,128)S(1)}, f32[16,32,1]{2,1,0:T(8,128)S(1)}, u32[]{:S(2)}, u32[]{:S(2)}) collective-permute-start(f32[16,32,1]{2,1,0:T(8,128)S(1)} %get-tuple-element.31), channel_id=1, source_target_pairs={{0,4},{4,8},{8,12},{12,16},{16,20},{20,24},{24,28},{28,0},{1,5},{5... | collective-permute-start | bytes 6152 | tf_op jit(solution)/shard_map/ppermute | solution.py:15
  113.8 9.1 %collective-permute-start.13 = (f32[16,32,1]{2,1,0:T(8,128)S(1)}, f32[16,32,1]{2,1,0:T(8,128)S(1)}, u32[]{:S(2)}, u32[]{:S(2)}) collective-permute-start(f32[16,32,1]{2,1,0:T(8,128)S(1)} %get-tuple-element.32), channel_id=1, source_target_pairs={{4,0},{8,4},{12,8},{16,12},{20,16},{24,20},{28,24},{0,28},{5,1},{9... | collective-permute-start | bytes 6152 | tf_op jit(solution)/shard_map/ppermute | solution.py:18
  123.0 4.8 %collective-permute-start.14 = (f32[16,1,258]{2,1,0:T(1,128)S(1)}, f32[16,1,258]{2,1,0:T(1,128)S(1)}, u32[]{:S(2)}, u32[]{:S(2)}) collective-permute-start(f32[16,1,258]{2,1,0:T(1,128)S(1)} %get-tuple-element.15), channel_id=1, source_target_pairs={{0,1},{1,2},{2,3},{3,0},{4,5},{5,6},{6,7},{7,4},{8,9},{9,10},{10,1... | collective-permute-start | bytes 49544 | tf_op jit(solution)/shard_map/ppermute | solution.py:15
  130.5 8.2 %collective-permute-start.16 = (f32[16,32,1]{2,1,0:T(8,128)S(1)}, f32[16,32,1]{2,1,0:T(8,128)S(1)}, u32[]{:S(2)}, u32[]{:S(2)}) collective-permute-start(f32[16,32,1]{2,1,0:T(8,128)S(1)} %get-tuple-element.29), channel_id=1, source_target_pairs={{0,4},{4,8},{8,12},{12,16},{16,20},{20,24},{24,28},{28,0},{1,5},{5... | collective-permute-start | bytes 6152 | tf_op jit(solution)/shard_map/ppermute | solution.py:15
  130.6 8.2 %collective-permute-start.17 = (f32[16,32,1]{2,1,0:T(8,128)S(1)}, f32[16,32,1]{2,1,0:T(8,128)S(1)}, u32[]{:S(2)}, u32[]{:S(2)}) collective-permute-start(f32[16,32,1]{2,1,0:T(8,128)S(1)} %get-tuple-element.30), channel_id=1, source_target_pairs={{4,0},{8,4},{12,8},{16,12},{20,16},{24,20},{28,24},{0,28},{5,1},{9... | collective-permute-start | bytes 6152 | tf_op jit(solution)/shard_map/ppermute | solution.py:18
  139.0 4.8 %collective-permute-start.18 = (f32[16,1,258]{2,1,0:T(1,128)S(1)}, f32[16,1,258]{2,1,0:T(1,128)S(1)}, u32[]{:S(2)}, u32[]{:S(2)}) collective-permute-start(f32[16,1,258]{2,1,0:T(1,128)S(1)} %get-tuple-element.13), channel_id=1, source_target_pairs={{0,1},{1,2},{2,3},{3,0},{4,5},{5,6},{6,7},{7,4},{8,9},{9,10},{10,1... | collective-permute-start | bytes 49544 | tf_op jit(solution)/shard_map/ppermute | solution.py:15
  146.3 9.1 %collective-permute-start.20 = (f32[16,32,1]{2,1,0:T(8,128)S(1)}, f32[16,32,1]{2,1,0:T(8,128)S(1)}, u32[]{:S(2)}, u32[]{:S(2)}) collective-permute-start(f32[16,32,1]{2,1,0:T(8,128)S(1)} %get-tuple-element.27), channel_id=1, source_target_pairs={{0,4},{4,8},{8,12},{12,16},{16,20},{20,24},{24,28},{28,0},{1,5},{5... | collective-permute-start | bytes 6152 | tf_op jit(solution)/shard_map/ppermute | solution.py:15
  146.4 9.1 %collective-permute-start.21 = (f32[16,32,1]{2,1,0:T(8,128)S(1)}, f32[16,32,1]{2,1,0:T(8,128)S(1)}, u32[]{:S(2)}, u32[]{:S(2)}) collective-permute-start(f32[16,32,1]{2,1,0:T(8,128)S(1)} %get-tuple-element.28), channel_id=1, source_target_pairs={{4,0},{8,4},{12,8},{16,12},{20,16},{24,20},{28,24},{0,28},{5,1},{9... | collective-permute-start | bytes 6152 | tf_op jit(solution)/shard_map/ppermute | solution.py:18
  155.7 4.8 %collective-permute-start.22 = (f32[16,1,258]{2,1,0:T(1,128)S(1)}, f32[16,1,258]{2,1,0:T(1,128)S(1)}, u32[]{:S(2)}, u32[]{:S(2)}) collective-permute-start(f32[16,1,258]{2,1,0:T(1,128)S(1)} %get-tuple-element.11), channel_id=1, source_target_pairs={{0,1},{1,2},{2,3},{3,0},{4,5},{5,6},{6,7},{7,4},{8,9},{9,10},{10,1... | collective-permute-start | bytes 49544 | tf_op jit(solution)/shard_map/ppermute | solution.py:15
  163.1 8.2 %collective-permute-start.24 = (f32[16,32,1]{2,1,0:T(8,128)S(1)}, f32[16,32,1]{2,1,0:T(8,128)S(1)}, u32[]{:S(2)}, u32[]{:S(2)}) collective-permute-start(f32[16,32,1]{2,1,0:T(8,128)S(1)} %get-tuple-element.25), channel_id=1, source_target_pairs={{0,4},{4,8},{8,12},{12,16},{16,20},{20,24},{24,28},{28,0},{1,5},{5... | collective-permute-start | bytes 6152 | tf_op jit(solution)/shard_map/ppermute | solution.py:15
  163.2 8.2 %collective-permute-start.25 = (f32[16,32,1]{2,1,0:T(8,128)S(1)}, f32[16,32,1]{2,1,0:T(8,128)S(1)}, u32[]{:S(2)}, u32[]{:S(2)}) collective-permute-start(f32[16,32,1]{2,1,0:T(8,128)S(1)} %get-tuple-element.26), channel_id=1, source_target_pairs={{4,0},{8,4},{12,8},{16,12},{20,16},{24,20},{28,24},{0,28},{5,1},{9... | collective-permute-start | bytes 6152 | tf_op jit(solution)/shard_map/ppermute | solution.py:18
  171.6 4.8 %collective-permute-start.26 = (f32[16,1,258]{2,1,0:T(1,128)S(1)}, f32[16,1,258]{2,1,0:T(1,128)S(1)}, u32[]{:S(2)}, u32[]{:S(2)}) collective-permute-start(f32[16,1,258]{2,1,0:T(1,128)S(1)} %get-tuple-element.9), channel_id=1, source_target_pairs={{0,1},{1,2},{2,3},{3,0},{4,5},{5,6},{6,7},{7,4},{8,9},{9,10},{10,1... | collective-permute-start | bytes 49544 | tf_op jit(solution)/shard_map/ppermute | solution.py:15
  174.0 3.8 %collective-permute-start.27 = (f32[16,1,258]{2,1,0:T(1,128)S(1)}, f32[16,1,258]{2,1,0:T(1,128)S(1)}, u32[]{:S(2)}, u32[]{:S(2)}) collective-permute-start(f32[16,1,258]{2,1,0:T(1,128)S(1)} %get-tuple-element.10), channel_id=1, source_target_pairs={{1,0},{2,1},{3,2},{0,3},{5,4},{6,5},{7,6},{4,7},{9,8},{10,9},{11,1... | collective-permute-start | bytes 49544 | tf_op jit(solution)/shard_map/ppermute | solution.py:18
  180.0 9.1 %collective-permute-start.28 = (f32[16,32,1]{2,1,0:T(8,128)S(1)}, f32[16,32,1]{2,1,0:T(8,128)S(1)}, u32[]{:S(2)}, u32[]{:S(2)}) collective-permute-start(f32[16,32,1]{2,1,0:T(8,128)S(1)} %get-tuple-element.23), channel_id=1, source_target_pairs={{0,4},{4,8},{8,12},{12,16},{16,20},{20,24},{24,28},{28,0},{1,5},{5... | collective-permute-start | bytes 6152 | tf_op jit(solution)/shard_map/ppermute | solution.py:15
  180.0 9.1 %collective-permute-start.29 = (f32[16,32,1]{2,1,0:T(8,128)S(1)}, f32[16,32,1]{2,1,0:T(8,128)S(1)}, u32[]{:S(2)}, u32[]{:S(2)}) collective-permute-start(f32[16,32,1]{2,1,0:T(8,128)S(1)} %get-tuple-element.24), channel_id=1, source_target_pairs={{4,0},{8,4},{12,8},{16,12},{20,16},{24,20},{28,24},{0,28},{5,1},{9... | collective-permute-start | bytes 6152 | tf_op jit(solution)/shard_map/ppermute | solution.py:18
  189.3 4.8 %collective-permute-start.30 = (f32[16,1,258]{2,1,0:T(1,128)S(1)}, f32[16,1,258]{2,1,0:T(1,128)S(1)}, u32[]{:S(2)}, u32[]{:S(2)}) collective-permute-start(f32[16,1,258]{2,1,0:T(1,128)S(1)} %get-tuple-element.7), channel_id=1, source_target_pairs={{0,1},{1,2},{2,3},{3,0},{4,5},{5,6},{6,7},{7,4},{8,9},{9,10},{10,1... | collective-permute-start | bytes 49544 | tf_op jit(solution)/shard_map/ppermute | solution.py:15
  190.8 3.8 %collective-permute-start.31 = (f32[16,1,258]{2,1,0:T(1,128)S(1)}, f32[16,1,258]{2,1,0:T(1,128)S(1)}, u32[]{:S(2)}, u32[]{:S(2)}) collective-permute-start(f32[16,1,258]{2,1,0:T(1,128)S(1)} %get-tuple-element.8), channel_id=1, source_target_pairs={{1,0},{2,1},{3,2},{0,3},{5,4},{6,5},{7,6},{4,7},{9,8},{10,9},{11,1... | collective-permute-start | bytes 49544 | tf_op jit(solution)/shard_map/ppermute | solution.py:18
  196.8 8.2 %collective-permute-start.32 = (f32[16,32,1]{2,1,0:T(8,128)S(1)}, f32[16,32,1]{2,1,0:T(8,128)S(1)}, u32[]{:S(2)}, u32[]{:S(2)}) collective-permute-start(f32[16,32,1]{2,1,0:T(8,128)S(1)} %get-tuple-element.21), channel_id=1, source_target_pairs={{0,4},{4,8},{8,12},{12,16},{16,20},{20,24},{24,28},{28,0},{1,5},{5... | collective-permute-start | bytes 6152 | tf_op jit(solution)/shard_map/ppermute | solution.py:15
  196.8 8.2 %collective-permute-start.33 = (f32[16,32,1]{2,1,0:T(8,128)S(1)}, f32[16,32,1]{2,1,0:T(8,128)S(1)}, u32[]{:S(2)}, u32[]{:S(2)}) collective-permute-start(f32[16,32,1]{2,1,0:T(8,128)S(1)} %get-tuple-element.22), channel_id=1, source_target_pairs={{4,0},{8,4},{12,8},{16,12},{20,16},{24,20},{28,24},{0,28},{5,1},{9... | collective-permute-start | bytes 6152 | tf_op jit(solution)/shard_map/ppermute | solution.py:18
  205.2 4.8 %collective-permute-start.34 = (f32[16,1,258]{2,1,0:T(1,128)S(1)}, f32[16,1,258]{2,1,0:T(1,128)S(1)}, u32[]{:S(2)}, u32[]{:S(2)}) collective-permute-start(f32[16,1,258]{2,1,0:T(1,128)S(1)} %get-tuple-element.5), channel_id=1, source_target_pairs={{0,1},{1,2},{2,3},{3,0},{4,5},{5,6},{6,7},{7,4},{8,9},{9,10},{10,1... | collective-permute-start | bytes 49544 | tf_op jit(solution)/shard_map/ppermute | solution.py:15
  (13 other events, 200.9 us)
where the time goes:
time: 214 us; the launch traced here: 213 us
  waiting for transfers between devices  73.4 us (34%)
  starting transfers between devices  68.9 us (32%)
  other arithmetic  46.7 us (22%)
  local copies, waits for them, and re-layouts  23.6 us (11%)
    ppermute x18, waiting for transfers between devices, with_halo(): lax.ppermute(lax.slice_in_dim(block, block.shape[dim] - width, None, axis...  57.5 us
    ppermute x18, starting transfers between devices, with_halo(): lax.ppermute(lax.slice_in_dim(block, 0, width, axis=dim), axis, backward)  42.7 us
    scatter-add x1, other arithmetic, body(): jnp.zeros((levels, rows_here * cols_here), jnp.float32).at[:, targets]  24.6 us
    ppermute x18, starting transfers between devices, with_halo(): lax.ppermute(lax.slice_in_dim(block, block.shape[dim] - width, None, axis...  16.5 us
    gather x2, local copies, waits for them, and re-layouts, body(): at_column = jnp.take(columns, targets, axis=1)  13.6 us
    ppermute x18, waiting for transfers between devices, with_halo(): lax.ppermute(lax.slice_in_dim(block, 0, width, axis=dim), axis, backward)  6.92 us
    all_to_all x1, starting transfers between devices, body(): lax.all_to_all(at_column, 'lon', split_axis=1, concat_axis=1, tiled=True)  6.33 us
    mul x8, other arithmetic, one_pass(): flux_north = north_face * (layer_field[:, 1:, :] - layer_field[:, :-1, :])  5.55 us
  transfers between devices with their start and end apart: 38, of which 28 were waited for; matrix products, arithmetic and copies ran while one was open for 2% of the time, Pallas kernels for 0%

commit v1 on v0

v1 whole, which is shorter than its diff:
```python
import functools

import jax
import jax.numpy as jnp
from jax import lax
from jax.experimental import pallas as pl
from jax.experimental.pallas import tpu as pltpu
from jax.sharding import PartitionSpec as P

PASSES = 8
MESH = pl.DeviceIdType.MESH
F32 = jnp.float32
BF16 = jnp.bfloat16


def pieces_of(x):
    first = x.astype(BF16)
    rest = x - first.astype(F32)
    second = rest.astype(BF16)
    third = (rest - second.astype(F32)).astype(BF16)
    return first, second, third


def kernel(
    n_lon, n_lat,
    state_ref, coef_lon_ref, coef_lat_ref, land_ref, cols_ref, count_ref, value_ref, weight_ref,
    out_ref,
    recv, seen, hot, spread, spread_bf, pieces, scattered, coefs, coef_out, coef_west, coef_east,
    east_b, north_b, field, edge_out, edge_west, edge_east,
    own_sem, send_sem, recv_sem, csend_sem, crecv_sem, gsend_sem, grecv_sem,
):
    levels, rows, cols = state_ref.shape
    halo = PASSES
    ext = rows + 2 * halo
    lanes = cols + 128
    cap = recv.shape[3]
    lon = lax.axis_index("lon")
    lat = lax.axis_index("lat")
    east, west = lax.rem(lon + 1, n_lon), lax.rem(lon + n_lon - 1, n_lon)
    north, south = lax.rem(lat + 1, n_lat), lax.rem(lat + n_lat - 1, n_lat)

    def at(lon_to, lat_to):
        return {"lon": lon_to, "lat": lat_to}

    around = [
        at(lon, north), at(lon, south), at(east, lat), at(west, lat),
        at(east, north), at(west, north), at(east, south), at(west, south),
    ]
    barrier = pltpu.get_barrier_semaphore()
    for step in range(1, n_lon):
        pl.semaphore_signal(
            barrier, inc=1, device_id=at(lax.rem(lon + step, n_lon), lat), device_id_type=MESH
        )
    for place in (0, 1, 4, 5, 6, 7):
        pl.semaphore_signal(barrier, inc=1, device_id=around[place], device_id_type=MESH)
    pl.semaphore_wait(barrier, n_lon - 1 + 6)

    sources = (value_ref, weight_ref)

    def profile_copy(which, step):
        peer = lax.rem(lon + step, n_lon)
        start = pl.multiple_of(peer * cap, 128)
        return pltpu.make_async_remote_copy(
            src_ref=sources[which].at[:, pl.ds(start, cap)],
            dst_ref=recv.at[which, step],
            send_sem=send_sem.at[which, step],
            recv_sem=recv_sem.at[which, step],
            device_id=at(peer, lat),
            device_id_type=MESH,
        )

    half = n_lon // 2
    order = []
    for off in range(half, 0, -1):
        order += [off] if 2 * off == n_lon else [off, n_lon - off]
    for step in order:
        for which in (0, 1):
            profile_copy(which, step).start()
    own = [
        pltpu.make_async_copy(
            sources[which].at[:, pl.ds(pl.multiple_of(lon * cap, 128), cap)],
            recv.at[which, 0],
            own_sem.at[which],
        )
        for which in (0, 1)
    ]
    for copy in own:
        copy.start()

    here = pl.ds(halo, rows)
    coefs[0, here, 0:cols] = land_ref[...].astype(F32)
    coefs[1, here, 0:cols] = coef_lon_ref[...]
    coefs[2, here, 0:cols] = coef_lat_ref[...]
    lane = lax.broadcasted_iota(jnp.int32, (rows, 128), 1)
    to_east = jnp.zeros((rows, 128), F32)
    to_west = jnp.zeros((rows, 128), F32)
    for a in range(3):
        low = coefs[a, here, 0:128]
        high = coefs[a, here, cols - 128:cols]
        mine = (lane >= 8 * a) & (lane < 8 * a + 8)
        to_east = jnp.where(mine, pltpu.roll(high, (8 * a + 8) % 128, axis=1), to_east)
        to_west = jnp.where(mine, low if a == 0 else pltpu.roll(low, 8 * a, axis=1), to_west)
    coef_out[0] = to_east
    coef_out[1] = to_west
    top, bottom = pl.ds(rows - halo, halo), pl.ds(0, halo)
    low_rim, high_rim = pl.ds(0, halo), pl.ds(halo + rows, halo)
    coef_moves = [
        (coefs.at[:, pl.ds(rows, halo), 0:cols], coefs.at[:, low_rim, 0:cols]),
        (coefs.at[:, pl.ds(halo, halo), 0:cols], coefs.at[:, high_rim, 0:cols]),
        (coef_out.at[0], coef_west.at[here]),
        (coef_out.at[1], coef_east.at[here]),
        (coef_out.at[0, top], coef_west.at[low_rim]),
        (coef_out.at[1, top], coef_east.at[low_rim]),
        (coef_out.at[0, bottom], coef_west.at[high_rim]),
        (coef_out.at[1, bottom], coef_east.at[high_rim]),
    ]
    coef_copies = [
        pltpu.make_async_remote_copy(
            src_ref=src, dst_ref=dst, send_sem=csend_sem.at[i], recv_sem=crecv_sem.at[i],
            device_id=around[i], device_id_type=MESH,
        )
        for i, (src, dst) in enumerate(coef_moves)
    ]
    for copy in coef_copies:
        copy.start()

    for r in range(rows):
        parts = pieces_of(state_ref[:, r, :])
        for i in range(3):
            pieces[i, levels * r:levels * (r + 1), :] = parts[i]

    def places(step):
        holder = lax.rem(lon + n_lon - step, n_lon)
        entry = cols_ref[:, pl.ds(pl.multiple_of(holder * cap, 128), cap)]
        return holder, entry // cols, entry % cols

    def gather_step(step, carry):
        _, row, col = places(step)
        which_col = lax.broadcasted_iota(jnp.int32, (cols, cap), 0)
        one_hot = jnp.where(which_col == col, 1.0, 0.0).astype(BF16)
        hot[step] = one_hot
        picked = jnp.dot(pieces[0], one_hot, preferred_element_type=F32)
        picked += jnp.dot(pieces[1], one_hot, preferred_element_type=F32)
        picked += jnp.dot(pieces[2], one_hot, preferred_element_type=F32)
        spread[...] = picked
        row_b = jnp.broadcast_to(row, (levels, cap))
        total = jnp.zeros((levels, cap), F32)
        for r in range(rows):
            total += jnp.where(row_b == r, spread[levels * r:levels * (r + 1), :], 0.0)
        seen[step] = total
        return carry

    lax.fori_loop(0, n_lon, gather_step, 0)

    for copy in coef_copies:
        copy.wait()
    lane_e = lax.broadcasted_iota(jnp.int32, (ext, 128), 1)
    from_west, from_east = coef_west[...], coef_east[...]
    for a in range(3):
        eastern = from_east if a == 0 else pltpu.roll(from_east, 128 - 8 * a, axis=1)
        western = pltpu.roll(from_west, 120 - 8 * a, axis=1)
        coefs[a, :, cols:lanes] = jnp.where(
            lane_e < 8, eastern, jnp.where(lane_e >= 120, western, 0.0)
        )
    row_place = lax.broadcasted_iota(jnp.int32, (ext, lanes), 0)
    first_out = jnp.where(lat == 0, halo, 0)
    last_out = jnp.where(lat == n_lat - 1, halo + rows, ext)
    inside = (row_place >= first_out) & (row_place < last_out)
    sea = jnp.where(inside, coefs[0], 0.0)
    coefs[0] = sea
    east_face = coefs[1] * sea * pltpu.roll(sea, lanes - 1, axis=1)
    north_face = coefs[2] * sea * pltpu.roll(sea, ext - 1, axis=0)
    for e in range(ext):
        east_b[e] = jnp.broadcast_to(east_face[e:e + 1, :], (8, lanes))
        north_b[e] = jnp.broadcast_to(north_face[e:e + 1, :], (8, lanes))

    scattered[...] = jnp.zeros_like(scattered)

    def scatter_step(step, carry):
        holder, row, _ = places(step)
        for which in (0, 1):

            @pl.when(step == 0)
            def _():
                own[which].wait()

            @pl.when(step != 0)
            def _():
                profile_copy(which, step).wait_recv()

        slot = lax.broadcasted_iota(jnp.int32, (levels, cap), 1)
        usable = jnp.where(slot < count_ref[0, holder], 1.0, 0.0)
        weighted = recv[1, step] * (recv[0, step] - seen[step]) * usable
        parts = pieces_of(weighted)
        row_b = jnp.broadcast_to(row, (levels, cap))
        for r in range(rows):
            mine = jnp.where(row_b == r, 1.0, 0.0).astype(BF16)
            for i in range(3):
                spread_bf[i, levels * r:levels * (r + 1), :] = mine * parts[i]
        one_hot = hot[step]
        dims = (((1,), (1,)), ((), ()))
        total = lax.dot_general(spread_bf[0], one_hot, dims, preferred_element_type=F32)
        total += lax.dot_general(spread_bf[1], one_hot, dims, preferred_element_type=F32)
        total += lax.dot_general(spread_bf[2], one_hot, dims, preferred_element_type=F32)
        scattered[...] += total
        return carry

    lax.fori_loop(0, n_lon, scatter_step, 0)

    for r in range(rows):
        sea_r = jnp.broadcast_to(coefs[0, halo + r:halo + r + 1, 0:cols], (levels, cols))
        field[0, halo + r, :, 0:cols] = scattered[levels * r:levels * (r + 1), :] * sea_r
    group = 128 // halo
    blocks = rows // group
    lane_g = lax.broadcasted_iota(jnp.int32, (levels, 128), 1)
    for j in range(blocks):
        to_east = jnp.zeros((levels, 128), F32)
        to_west = jnp.zeros((levels, 128), F32)
        for k in range(group):
            low = field[0, halo + j * group + k, :, 0:128]
            high = field[0, halo + j * group + k, :, cols - 128:cols]
            mine = (lane_g >= 8 * k) & (lane_g < 8 * k + 8)
            to_east = jnp.where(mine, pltpu.roll(high, (8 * k + 8) % 128, axis=1) if k < group - 1 else high, to_east)
            to_west = jnp.where(mine, low if k == 0 else pltpu.roll(low, 8 * k, axis=1), to_west)
        edge_out[0, j] = to_east
        edge_out[1, j] = to_west
    middle = pl.ds(1, blocks)
    field_moves = [
        (field.at[0, pl.ds(rows, halo), :, 0:cols], field.at[0, low_rim, :, 0:cols]),
        (field.at[0, pl.ds(halo, halo), :, 0:cols], field.at[0, high_rim, :, 0:cols]),
        (edge_out.at[0], edge_west.at[middle]),
        (edge_out.at[1], edge_east.at[middle]),
        (edge_out.at[0, blocks - 1], edge_west.at[0]),
        (edge_out.at[1, blocks - 1], edge_east.at[0]),
        (edge_out.at[0, 0], edge_west.at[blocks + 1]),
        (edge_out.at[1, 0], edge_east.at[blocks + 1]),
    ]
    field_copies = [
        pltpu.make_async_remote_copy(
            src_ref=src, dst_ref=dst, send_sem=gsend_sem.at[i], recv_sem=grecv_sem.at[i],
            device_id=around[i], device_id_type=MESH,
        )
        for i, (src, dst) in enumerate(field_moves)
    ]
    for i in (2, 3, 0, 1, 4, 5, 6, 7):
        field_copies[i].start()

    def unpack(first, last):
        for e in range(first, last):
            j, k = (e + halo) // group, (e + halo) % group
            eastern = edge_east[j]
            if k > 0:
                eastern = pltpu.roll(eastern, 128 - 8 * k, axis=1)
            western = edge_west[j]
            if k < group - 1:
                western = pltpu.roll(western, 120 - 8 * k, axis=1)
            field[0, e, :, cols:lanes] = jnp.where(
                lane_g < 8, eastern, jnp.where(lane_g >= 120, western, 0.0)
            )

    def twice(face):
        return jnp.concatenate([face] * (levels // 8), axis=0)

    def advance(t, first, last):
        before = field.at[t - 1]
        start = before[first]
        flux_in = twice(north_b[first - 1]) * (start - before[first - 1])

        def row_step(e, carry):
            g, flux_south = carry
            g_north = before[e + 1]
            flux_north = twice(north_b[e]) * (g_north - g)
            flux_east = twice(east_b[e]) * (pltpu.roll(g, lanes - 1, axis=1) - g)
            new = g + flux_east - pltpu.roll(flux_east, 1, axis=1) + flux_north - flux_south
            if t == PASSES:
                out_ref[e - halo] = new[:, 0:cols]
            else:
                field[t, e] = new
            return g_north, flux_north

        lax.fori_loop(first, last, row_step, (start, flux_in), unroll=2)

    field_copies[2].wait_recv()
    field_copies[3].wait_recv()
    unpack(halo, halo + rows)
    for t in range(1, PASSES + 1):
        advance(t, halo + t, halo + rows - t)
    for i in (0, 1, 4, 5, 6, 7):
        field_copies[i].wait_recv()
    unpack(0, halo)
    unpack(halo + rows, ext)
    for t in range(1, PASSES + 1):
        advance(t, t, halo + t)
        advance(t, halo + rows - t, ext - t)

    for step in order:
        for which in (0, 1):
            profile_copy(which, step).wait_send()
    for copy in field_copies:
        copy.wait_send()


def body(state, coef_lon, coef_lat, land_sea, send_cols, send_count, obs_value, obs_weight):
    levels, rows, cols = state.shape
    n_lon = lax.axis_size("lon")
    n_lat = lax.axis_size("lat")
    slots = send_cols.shape[1]
    cap = slots // n_lon
    ext, lanes = rows + 2 * PASSES, cols + 128
    blocks = rows * PASSES // 128
    vmem = pl.BlockSpec(memory_space=pltpu.VMEM)
    anywhere = pl.BlockSpec(memory_space=pl.ANY)
    dma = pltpu.SemaphoreType.DMA
    out = pl.pallas_call(
        functools.partial(kernel, n_lon, n_lat),
        out_shape=jax.ShapeDtypeStruct((rows, levels, cols), F32),
        in_specs=[vmem] * 5 + [pl.BlockSpec(memory_space=pltpu.SMEM)] + [anywhere] * 2,
        out_specs=vmem,
        scratch_shapes=[
            pltpu.VMEM((2, n_lon, levels, cap), F32),
            pltpu.VMEM((n_lon, levels, cap), F32),
            pltpu.VMEM((n_lon, cols, cap), BF16),
            pltpu.VMEM((rows * levels, cap), F32),
            pltpu.VMEM((3, rows * levels, cap), BF16),
            pltpu.VMEM((3, rows * levels, cols), BF16),
            pltpu.VMEM((rows * levels, cols), F32),
            pltpu.VMEM((3, ext, lanes), F32),
            pltpu.VMEM((2, rows, 128), F32),
            pltpu.VMEM((ext, 128), F32),
            pltpu.VMEM((ext, 128), F32),
            pltpu.VMEM((ext, 8, lanes), F32),
            pltpu.VMEM((ext, 8, lanes), F32),
            pltpu.VMEM((PASSES, ext, levels, lanes), F32),
            pltpu.VMEM((2, blocks, levels, 128), F32),
            pltpu.VMEM((blocks + 2, levels, 128), F32),
            pltpu.VMEM((blocks + 2, levels, 128), F32),
            dma((2,)),
            dma((2, n_lon)),
            dma((2, n_lon)),
            dma((8,)),
            dma((8,)),
            dma((8,)),
            dma((8,)),
        ],
        compiler_params=pltpu.CompilerParams(
            collective_id=0, has_side_effects=True, vmem_limit_bytes=48 * 2**20
        ),
        name="analysis",
    )(
        state, coef_lon, coef_lat, land_sea, send_cols, send_count,
        obs_value.reshape(levels, slots), obs_weight.reshape(levels, slots),
    )
    return jnp.transpose(out, (1, 0, 2))


def solution(mesh):
    placed = (
        P(None, "lat", "lon"),
        P("lat", "lon"),
        P("lat", "lon"),
        P("lat", "lon"),
        P("lat", "lon"),
        P("lat", "lon"),
        P(None, "lat", "lon"),
        P(None, "lat", "lon"),
    )
    return jax.shard_map(
        body, mesh=mesh, in_specs=placed, out_specs=P(None, "lat", "lon"), check_vma=False
    )
```

time: 214 us -> 56.1 us (0.26)
  waiting for transfers between devices: 73.4 us -> 0 us
  starting transfers between devices: 68.9 us -> 0 us
  Pallas kernels: 0 us -> 52.8 us
  other arithmetic: 46.7 us -> 0 us
  local copies, waits for them, and re-layouts: 23.6 us -> 3.12 us
    ppermute x36 -> x0, waiting for transfers between devices: 64.5 us -> none  [the longest x18 57.5 us: with_halo(): lax.ppermute(lax.slice_in_dim(block, block.shape[dim] - width, None, axis...]
    ppermute x36 -> x0, starting transfers between devices: 59.2 us -> none  [the longest x18 42.7 us: with_halo(): lax.ppermute(lax.slice_in_dim(block, 0, width, axis=dim), axis, backward)]
    pallas_call x0 -> x1, Pallas kernels: none -> 52.8 us  [body(): pl.pallas_call(functools.partial(kernel, n_lon, n_lat), out_shape=jax.Sha...]
    scatter-add x1 -> x0, other arithmetic: 24.6 us -> none  [body(): jnp.zeros((levels, rows_here * cols_here), jnp.float32).at[:, targets]]
    gather x2 -> x0, local copies, waits for them, and re-layouts: 13.6 us -> none  [body(): at_column = jnp.take(columns, targets, axis=1)]
    all_to_all x2 -> x0, starting transfers between devices: 9.74 us -> none  [the longest x1 6.33 us: body(): lax.all_to_all(at_column, 'lon', split_axis=1, concat_axis=1, tiled=True)]
    all_to_all x2 -> x0, waiting for transfers between devices: 8.95 us -> none  [the longest x1 4.79 us: body(): lax.all_to_all(at_column, 'lon', split_axis=1, concat_axis=1, tiled=True)]
    mul x22 -> x0, other arithmetic: 8.67 us -> none  [the longest x8 5.55 us: one_pass(): flux_north = north_face * (layer_field[:, 1:, :] - layer_field[:, :-1, :])]
  transfers between devices with their start and end apart: 38 -> 0, of which waited for: 28 -> 0; matrix products, arithmetic and copies ran while one was open for 2% -> 0% of each run, Pallas kernels for 0% -> 0%
where the time goes in v1:
time: 56.1 us; the launch traced here: 55.9 us
  Pallas kernels  52.8 us (94%)
  local copies, waits for them, and re-layouts  3.12 us (6%)
    pallas_call x1, Pallas kernels, body(): pl.pallas_call(functools.partial(kernel, n_lon, n_lat), out_shape=jax.Sha...  52.8 us
    unnamed x13, local copies, waits for them, and re-layouts  2.02 us

profile of v1, /device:TPU:0, one launch (start us, length us, event | category | flops | bytes accessed | tf_op | source)
XLA Modules:
  0.0 55.9 jit_solution(5201644102189006830)
XLA Ops:
  0.0 0.0 copy-start.4
  0.0 0.0 copy-start.3
  0.0 0.0 copy-start.2
  0.0 0.0 copy-start.1
  0.0 0.0 copy-start
  0.0 1.4 %copy_bitcast_fusion = (f32[16,4096]{1,0:T(8,128)S(1)}, f32[16,4096]{1,0:T(8,128)S(1)}) fusion(f32[16,1,4096]{2,1,0:T(1,128)} %param.15, f32[16,1,4096]{2,1,0:T(1,128)} %param.14), kind=kLoop, calls=%fused_computation | loop fusion | bytes 1048576
  1.4 0.0 copy-start.5
  1.4 0.0 copy-done.4
  1.4 0.0 copy-done.3
  1.4 0.0 copy-done.2
  1.5 0.0 copy-done.1
  1.5 0.0 copy-done
  1.5 0.6 %copy-done.5 = s32[1,8]{1,0:T(1,128)S(1)} copy-done((s32[1,8]{1,0:T(1,128)S(1)}, s32[1,8]{1,0:T(1,128)}, u32[]{:S(2)}) %copy-start.5) | copy-done | bytes 56
  2.1 52.8 %analysis.1 = f32[32,16,256]{2,1,0:T(8,128)S(1)} custom-call(f32[16,32,256]{2,1,0:T(8,128)S(1)} %copy-done, f32[32,256]{1,0:T(8,128)S(1)} %copy-done.1, f32[32,256]{1,0:T(8,128)S(1)} %copy-done.2, s32[32,256]{1,0:T(8,128)S(1)} %copy-done.3, s32[1,4096]{1,0:T(1,128)S(1)} %copy-done.4, s32[1,8]{1,0:T(1,128)S(1)} %copy-done.5, ...), custom_call_target="tpu_custom_call" | custom-call | tf_op jit(solution)/shard_map/analysis/pallas_call | solution.py:314
  54.8 1.1 %copy.9 = f32[16,32,256]{2,1,0:T(8,128)} copy(f32[16,32,256]{2,0,1:T(8,128)S(1)} %bitcast.5) | data formatting | bytes 1048576 | tf_op jit(solution)/shard_map/transpose | solution.py:353
Async XLA Ops:
  0.0 1.4 %copy-start.4 = (s32[1,4096]{1,0:T(1,128)S(1)}, s32[1,4096]{1,0:T(1,128)}, u32[]{:S(2)}) copy-start(s32[1,4096]{1,0:T(1,128)} %cols_ref.1) | copy-start | bytes 49156
  0.0 1.4 %copy-start.3 = (s32[32,256]{1,0:T(8,128)S(1)}, s32[32,256]{1,0:T(8,128)}, u32[]{:S(2)}) copy-start(s32[32,256]{1,0:T(8,128)} %land_ref.1) | copy-start | bytes 98308
  0.0 1.4 %copy-start.2 = (f32[32,256]{1,0:T(8,128)S(1)}, f32[32,256]{1,0:T(8,128)}, u32[]{:S(2)}) copy-start(f32[32,256]{1,0:T(8,128)} %coef_lat_ref.1) | copy-start | bytes 98308
  0.0 1.4 %copy-start.1 = (f32[32,256]{1,0:T(8,128)S(1)}, f32[32,256]{1,0:T(8,128)}, u32[]{:S(2)}) copy-start(f32[32,256]{1,0:T(8,128)} %coef_lon_ref.1) | copy-start | bytes 98308
  0.0 1.5 %copy-start = (f32[16,32,256]{2,1,0:T(8,128)S(1)}, f32[16,32,256]{2,1,0:T(8,128)}, u32[]{:S(2)}) copy-start(f32[16,32,256]{2,1,0:T(8,128)} %state_ref.1) | copy-start | bytes 1572868
  1.4 0.7 %copy-start.5 = (s32[1,8]{1,0:T(1,128)S(1)}, s32[1,8]{1,0:T(1,128)}, u32[]{:S(2)}) copy-start(s32[1,8]{1,0:T(1,128)} %count_ref.1) | copy-start | bytes 100

commit v2 on v1

--- a/solution.py
+++ b/solution.py
@@ -26,7 +26,7 @@
     state_ref, coef_lon_ref, coef_lat_ref, land_ref, cols_ref, count_ref, value_ref, weight_ref,
     out_ref,
     recv, seen, hot, spread, spread_bf, pieces, scattered, coefs, coef_out, coef_west, coef_east,
-    east_b, north_b, field, edge_out, edge_west, edge_east,
+    east_b, west_b, north_b, field, edge_out, edge_west, edge_east,
     own_sem, send_sem, recv_sem, csend_sem, crecv_sem, gsend_sem, grecv_sem,
 ):
     levels, rows, cols = state_ref.shape
@@ -132,7 +132,7 @@
     def places(step):
         holder = lax.rem(lon + n_lon - step, n_lon)
         entry = cols_ref[:, pl.ds(pl.multiple_of(holder * cap, 128), cap)]
-        return holder, entry // cols, entry % cols
+        return holder, lax.shift_right_logical(entry, cols.bit_length() - 1), entry & (cols - 1)
 
     def gather_step(step, carry):
         _, row, col = places(step)
@@ -170,13 +170,16 @@
     coefs[0] = sea
     east_face = coefs[1] * sea * pltpu.roll(sea, lanes - 1, axis=1)
     north_face = coefs[2] * sea * pltpu.roll(sea, ext - 1, axis=0)
+    west_face = pltpu.roll(east_face, 1, axis=1)
     for e in range(ext):
+        west_b[e] = jnp.broadcast_to(west_face[e:e + 1, :], (8, lanes))
         east_b[e] = jnp.broadcast_to(east_face[e:e + 1, :], (8, lanes))
         north_b[e] = jnp.broadcast_to(north_face[e:e + 1, :], (8, lanes))
 
     scattered[...] = jnp.zeros_like(scattered)
 
-    def scatter_step(step, carry):
+    def scatter_step(turn, carry):
+        step = jnp.where(turn % 2 == 1, (turn + 1) // 2, (n_lon - turn // 2) % n_lon)
         holder, row, _ = places(step)
         for which in (0, 1):
 
@@ -262,23 +265,19 @@
         return jnp.concatenate([face] * (levels // 8), axis=0)
 
     def advance(t, first, last):
-        before = field.at[t - 1]
-        start = before[first]
-        flux_in = twice(north_b[first - 1]) * (start - before[first - 1])
-
-        def row_step(e, carry):
-            g, flux_south = carry
-            g_north = before[e + 1]
+        g = field[t - 1, first]
+        flux_south = twice(north_b[first - 1]) * (g - field[t - 1, first - 1])
+        for e in range(first, last):
+            g_north = field[t - 1, e + 1]
             flux_north = twice(north_b[e]) * (g_north - g)
             flux_east = twice(east_b[e]) * (pltpu.roll(g, lanes - 1, axis=1) - g)
-            new = g + flux_east - pltpu.roll(flux_east, 1, axis=1) + flux_north - flux_south
+            flux_west = twice(west_b[e]) * (g - pltpu.roll(g, 1, axis=1))
+            new = g + flux_east - flux_west + flux_north - flux_south
             if t == PASSES:
                 out_ref[e - halo] = new[:, 0:cols]
             else:
                 field[t, e] = new
-            return g_north, flux_north
-
-        lax.fori_loop(first, last, row_step, (start, flux_in), unroll=2)
+            g, flux_south = g_north, flux_north
 
     field_copies[2].wait_recv()
     field_copies[3].wait_recv()
@@ -330,6 +329,7 @@
             pltpu.VMEM((ext, 128), F32),
             pltpu.VMEM((ext, 8, lanes), F32),
             pltpu.VMEM((ext, 8, lanes), F32),
+            pltpu.VMEM((ext, 8, lanes), F32),
             pltpu.VMEM((PASSES, ext, levels, lanes), F32),
             pltpu.VMEM((2, blocks, levels, 128), F32),
             pltpu.VMEM((blocks + 2, levels, 128), F32),

time: 56.1 us -> 36.3 us (0.65)
  Pallas kernels: 52.8 us -> 32.6 us
    pallas_call x1, Pallas kernels: 52.8 us -> 32.6 us  [body(): pl.pallas_call(functools.partial(kernel, n_lon, n_lat), out_shape=jax.Sha...]
where the time goes in v2:
time: 36.3 us; the launch traced here: 35.8 us
  Pallas kernels  32.6 us (90%)
  local copies, waits for them, and re-layouts  3.12 us (9%)
    pallas_call x1, Pallas kernels, body(): pl.pallas_call(functools.partial(kernel, n_lon, n_lat), out_shape=jax.Sha...  32.6 us
    unnamed x13, local copies, waits for them, and re-layouts  2.02 us
    transpose x1, local copies, waits for them, and re-layouts, body(): return jnp.transpose(out, (1, 0, 2))  1.1 us

profile of v2, /device:TPU:0, one launch (start us, length us, event | category | flops | bytes accessed | tf_op | source)
XLA Modules:
  0.0 35.8 jit_solution(6706115149777997018)
XLA Ops:
  0.0 0.0 copy-start.4
  0.0 0.0 copy-start.3
  0.0 0.0 copy-start.2
  0.0 0.0 copy-start.1
  0.0 0.0 copy-start
  0.0 1.4 %copy_bitcast_fusion = (f32[16,4096]{1,0:T(8,128)S(1)}, f32[16,4096]{1,0:T(8,128)S(1)}) fusion(f32[16,1,4096]{2,1,0:T(1,128)} %param.15, f32[16,1,4096]{2,1,0:T(1,128)} %param.14), kind=kLoop, calls=%fused_computation | loop fusion | bytes 1048576
  1.4 0.0 copy-start.5
  1.4 0.0 copy-done.4
  1.4 0.0 copy-done.3
  1.4 0.0 copy-done.2
  1.5 0.0 copy-done.1
  1.5 0.0 copy-done
  1.5 0.6 %copy-done.5 = s32[1,8]{1,0:T(1,128)S(1)} copy-done((s32[1,8]{1,0:T(1,128)S(1)}, s32[1,8]{1,0:T(1,128)}, u32[]{:S(2)}) %copy-start.5) | copy-done | bytes 56
  2.1 32.6 %analysis.1 = f32[32,16,256]{2,1,0:T(8,128)S(1)} custom-call(f32[16,32,256]{2,1,0:T(8,128)S(1)} %copy-done, f32[32,256]{1,0:T(8,128)S(1)} %copy-done.1, f32[32,256]{1,0:T(8,128)S(1)} %copy-done.2, s32[32,256]{1,0:T(8,128)S(1)} %copy-done.3, s32[1,4096]{1,0:T(1,128)S(1)} %copy-done.4, s32[1,8]{1,0:T(1,128)S(1)} %copy-done.5, ...), custom_call_target="tpu_custom_call" | custom-call | tf_op jit(solution)/shard_map/analysis/pallas_call | solution.py:313
  34.7 1.1 %copy.9 = f32[16,32,256]{2,1,0:T(8,128)} copy(f32[16,32,256]{2,0,1:T(8,128)S(1)} %bitcast.5) | data formatting | bytes 1048576 | tf_op jit(solution)/shard_map/transpose | solution.py:353
Async XLA Ops:
  0.0 1.4 %copy-start.4 = (s32[1,4096]{1,0:T(1,128)S(1)}, s32[1,4096]{1,0:T(1,128)}, u32[]{:S(2)}) copy-start(s32[1,4096]{1,0:T(1,128)} %cols_ref.1) | copy-start | bytes 49156
  0.0 1.4 %copy-start.3 = (s32[32,256]{1,0:T(8,128)S(1)}, s32[32,256]{1,0:T(8,128)}, u32[]{:S(2)}) copy-start(s32[32,256]{1,0:T(8,128)} %land_ref.1) | copy-start | bytes 98308
  0.0 1.4 %copy-start.2 = (f32[32,256]{1,0:T(8,128)S(1)}, f32[32,256]{1,0:T(8,128)}, u32[]{:S(2)}) copy-start(f32[32,256]{1,0:T(8,128)} %coef_lat_ref.1) | copy-start | bytes 98308
  0.0 1.4 %copy-start.1 = (f32[32,256]{1,0:T(8,128)S(1)}, f32[32,256]{1,0:T(8,128)}, u32[]{:S(2)}) copy-start(f32[32,256]{1,0:T(8,128)} %coef_lon_ref.1) | copy-start | bytes 98308
  0.0 1.5 %copy-start = (f32[16,32,256]{2,1,0:T(8,128)S(1)}, f32[16,32,256]{2,1,0:T(8,128)}, u32[]{:S(2)}) copy-start(f32[16,32,256]{2,1,0:T(8,128)} %state_ref.1) | copy-start | bytes 1572868
  1.4 0.7 %copy-start.5 = (s32[1,8]{1,0:T(1,128)S(1)}, s32[1,8]{1,0:T(1,128)}, u32[]{:S(2)}) copy-start(s32[1,8]{1,0:T(1,128)} %count_ref.1) | copy-start | bytes 100

commit v3 on v2

--- a/solution.py
+++ b/solution.py
@@ -30,10 +30,11 @@
     own_sem, send_sem, recv_sem, csend_sem, crecv_sem, gsend_sem, grecv_sem,
 ):
     levels, rows, cols = state_ref.shape
+    cells = rows * levels
     halo = PASSES
     ext = rows + 2 * halo
     lanes = cols + 128
-    cap = recv.shape[3]
+    cap = recv.shape[4]
     lon = lax.axis_index("lon")
     lat = lax.axis_index("lat")
     east, west = lax.rem(lon + 1, n_lon), lax.rem(lon + n_lon - 1, n_lon)
@@ -53,39 +54,6 @@
         )
     for place in (0, 1, 4, 5, 6, 7):
         pl.semaphore_signal(barrier, inc=1, device_id=around[place], device_id_type=MESH)
-    pl.semaphore_wait(barrier, n_lon - 1 + 6)
-
-    sources = (value_ref, weight_ref)
-
-    def profile_copy(which, step):
-        peer = lax.rem(lon + step, n_lon)
-        start = pl.multiple_of(peer * cap, 128)
-        return pltpu.make_async_remote_copy(
-            src_ref=sources[which].at[:, pl.ds(start, cap)],
-            dst_ref=recv.at[which, step],
-            send_sem=send_sem.at[which, step],
-            recv_sem=recv_sem.at[which, step],
-            device_id=at(peer, lat),
-            device_id_type=MESH,
-        )
-
-    half = n_lon // 2
-    order = []
-    for off in range(half, 0, -1):
-        order += [off] if 2 * off == n_lon else [off, n_lon - off]
-    for step in order:
-        for which in (0, 1):
-            profile_copy(which, step).start()
-    own = [
-        pltpu.make_async_copy(
-            sources[which].at[:, pl.ds(pl.multiple_of(lon * cap, 128), cap)],
-            recv.at[which, 0],
-            own_sem.at[which],
-        )
-        for which in (0, 1)
-    ]
-    for copy in own:
-        copy.start()
 
     here = pl.ds(halo, rows)
     coefs[0, here, 0:cols] = land_ref[...].astype(F32)
@@ -102,6 +70,46 @@
         to_west = jnp.where(mine, low if a == 0 else pltpu.roll(low, 8 * a, axis=1), to_west)
     coef_out[0] = to_east
     coef_out[1] = to_west
+
+    for r in range(rows):
+        parts = pieces_of(state_ref[:, r, :])
+        for i in range(3):
+            pieces[cells * i + levels * r:cells * i + levels * (r + 1), :] = parts[i]
+
+    pl.semaphore_wait(barrier, n_lon - 1 + 6)
+
+    sources = (value_ref, weight_ref)
+
+    def profile_copy(which, step):
+        peer = lax.rem(lon + step, n_lon)
+        start = pl.multiple_of(peer * cap, 128)
+        return pltpu.make_async_remote_copy(
+            src_ref=sources[which].at[:, :, pl.ds(start, cap)],
+            dst_ref=recv.at[which, step],
+            send_sem=send_sem.at[which, step],
+            recv_sem=recv_sem.at[which, step],
+            device_id=at(peer, lat),
+            device_id_type=MESH,
+        )
+
+    half = n_lon // 2
+    order = []
+    for off in range(half, 0, -1):
+        order += [off] if 2 * off == n_lon else [off, n_lon - off]
+    for step in order:
+        for which in (0, 1):
+            profile_copy(which, step).start()
+    own = [
+        pltpu.make_async_copy(
+            sources[which].at[:, :, pl.ds(pl.multiple_of(lon * cap, 128), cap)],
+            recv.at[which, 0],
+            own_sem.at[which],
+        )
+        for which in (0, 1)
+    ]
+    for copy in own:
+        copy.start()
+
     top, bottom = pl.ds(rows - halo, halo), pl.ds(0, halo)
     low_rim, high_rim = pl.ds(0, halo), pl.ds(halo + rows, halo)
     coef_moves = [
@@ -124,11 +132,6 @@
     for copy in coef_copies:
         copy.start()
 
-    for r in range(rows):
-        parts = pieces_of(state_ref[:, r, :])
-        for i in range(3):
-            pieces[i, levels * r:levels * (r + 1), :] = parts[i]
-
     def places(step):
         holder = lax.rem(lon + n_lon - step, n_lon)
         entry = cols_ref[:, pl.ds(pl.multiple_of(holder * cap, 128), cap)]
@@ -139,15 +142,19 @@
         which_col = lax.broadcasted_iota(jnp.int32, (cols, cap), 0)
         one_hot = jnp.where(which_col == col, 1.0, 0.0).astype(BF16)
         hot[step] = one_hot
-        picked = jnp.dot(pieces[0], one_hot, preferred_element_type=F32)
-        picked += jnp.dot(pieces[1], one_hot, preferred_element_type=F32)
-        picked += jnp.dot(pieces[2], one_hot, preferred_element_type=F32)
-        spread[...] = picked
-        row_b = jnp.broadcast_to(row, (levels, cap))
-        total = jnp.zeros((levels, cap), F32)
+        spread[...] = jnp.dot(pieces[...], one_hot, preferred_element_type=F32)
+        row_b = jnp.broadcast_to(row, (8, cap))
+        totals = [jnp.zeros((8, cap), F32) for _ in range(0, levels, 8)]
         for r in range(rows):
-            total += jnp.where(row_b == r, spread[levels * r:levels * (r + 1), :], 0.0)
-        seen[step] = total
+            mine = row_b == r
+            for h in range(levels // 8):
+                at_row = pl.ds(levels * r + 8 * h, 8)
+                picked = spread[at_row, :]
+                for i in range(1, 3):
+                    picked += spread[pl.ds(cells * i + levels * r + 8 * h, 8), :]
+                totals[h] += jnp.where(mine, picked, 0.0)
+        for h in range(levels // 8):
+            seen[step, 8 * h:8 * h + 8] = totals[h]
         return carry
 
     lax.fori_loop(0, n_lon, gather_step, 0)
@@ -193,28 +200,50 @@
 
         slot = lax.broadcasted_iota(jnp.int32, (levels, cap), 1)
         usable = jnp.where(slot < count_ref[0, holder], 1.0, 0.0)
-        weighted = recv[1, step] * (recv[0, step] - seen[step]) * usable
-        parts = pieces_of(weighted)
-        row_b = jnp.broadcast_to(row, (levels, cap))
+        weighted = recv[1, step, :, 0, :] * (recv[0, step, :, 0, :] - seen[step]) * usable
+        parts = pieces_of(weighted)[:2]
+        row_b = jnp.broadcast_to(row.astype(F32), (levels, cap)).astype(BF16)
+        nothing = jnp.zeros((levels, cap), BF16)
         for r in range(rows):
-            mine = jnp.where(row_b == r, 1.0, 0.0).astype(BF16)
-            for i in range(3):
-                spread_bf[i, levels * r:levels * (r + 1), :] = mine * parts[i]
-        one_hot = hot[step]
-        dims = (((1,), (1,)), ((), ()))
-        total = lax.dot_general(spread_bf[0], one_hot, dims, preferred_element_type=F32)
-        total += lax.dot_general(spread_bf[1], one_hot, dims, preferred_element_type=F32)
-        total += lax.dot_general(spread_bf[2], one_hot, dims, preferred_element_type=F32)
-        scattered[...] += total
+            mine = row_b == jnp.asarray(r, BF16)
+            for i in range(2):
+                start = cells * i + levels * r
+                spread_bf[start:start + levels, :] = jnp.where(mine, parts[i], nothing)
+        total = lax.dot_general(
+            spread_bf[...], hot[step], (((1,), (1,)), ((), ())), preferred_element_type=F32
+        )
+        scattered[...] += total[:cells] + total[cells:]
         return carry
 
     lax.fori_loop(0, n_lon, scatter_step, 0)
 
-    for r in range(rows):
+    group = 128 // halo
+    blocks = rows // group
+    middle = pl.ds(1, blocks)
+    field_moves = [
+        (field.at[0, pl.ds(rows, halo), :, 0:cols], field.at[0, low_rim, :, 0:cols]),
+        (field.at[0, pl.ds(halo, halo), :, 0:cols], field.at[0, high_rim, :, 0:cols]),
+        (edge_out.at[0], edge_west.at[middle]),
+        (edge_out.at[1], edge_east.at[middle]),
+        (edge_out.at[0, blocks - 1], edge_west.at[0]),
+        (edge_out.at[1, blocks - 1], edge_east.at[0]),
+        (edge_out.at[0, 0], edge_west.at[blocks + 1]),
+        (edge_out.at[1, 0], edge_east.at[blocks + 1]),
+    ]
+    field_copies = [
+        pltpu.make_async_remote_copy(
+            src_ref=src, dst_ref=dst, send_sem=gsend_sem.at[i], recv_sem=grecv_sem.at[i],
+            device_id=around[i], device_id_type=MESH,
+        )
+        for i, (src, dst) in enumerate(field_moves)
+    ]
+    border = list(range(halo)) + list(range(rows - halo, rows))
+    for r in border + list(range(halo, rows - halo)):
+        if r == halo:
+            field_copies[0].start()
+            field_copies[1].start()
         sea_r = jnp.broadcast_to(coefs[0, halo + r:halo + r + 1, 0:cols], (levels, cols))
         field[0, halo + r, :, 0:cols] = scattered[levels * r:levels * (r + 1), :] * sea_r
-    group = 128 // halo
-    blocks = rows // group
     lane_g = lax.broadcasted_iota(jnp.int32, (levels, 128), 1)
     for j in range(blocks):
         to_east = jnp.zeros((levels, 128), F32)
@@ -227,25 +256,7 @@
             to_west = jnp.where(mine, low if k == 0 else pltpu.roll(low, 8 * k, axis=1), to_west)
         edge_out[0, j] = to_east
         edge_out[1, j] = to_west
-    middle = pl.ds(1, blocks)
-    field_moves = [
-        (field.at[0, pl.ds(rows, halo), :, 0:cols], field.at[0, low_rim, :, 0:cols]),
-        (field.at[0, pl.ds(halo, halo), :, 0:cols], field.at[0, high_rim, :, 0:cols]),
-        (edge_out.at[0], edge_west.at[middle]),
-        (edge_out.at[1], edge_east.at[middle]),
-        (edge_out.at[0, blocks - 1], edge_west.at[0]),
-        (edge_out.at[1, blocks - 1], edge_east.at[0]),
-        (edge_out.at[0, 0], edge_west.at[blocks + 1]),
-        (edge_out.at[1, 0], edge_east.at[blocks + 1]),
-    ]
-    field_copies = [
-        pltpu.make_async_remote_copy(
-            src_ref=src, dst_ref=dst, send_sem=gsend_sem.at[i], recv_sem=grecv_sem.at[i],
-            device_id=around[i], device_id_type=MESH,
-        )
-        for i, (src, dst) in enumerate(field_moves)
-    ]
-    for i in (2, 3, 0, 1, 4, 5, 6, 7):
+    for i in range(2, 8):
         field_copies[i].start()
 
     def unpack(first, last):
@@ -316,12 +327,12 @@
         in_specs=[vmem] * 5 + [pl.BlockSpec(memory_space=pltpu.SMEM)] + [anywhere] * 2,
         out_specs=vmem,
         scratch_shapes=[
-            pltpu.VMEM((2, n_lon, levels, cap), F32),
+            pltpu.VMEM((2, n_lon, levels, 1, cap), F32),
             pltpu.VMEM((n_lon, levels, cap), F32),
             pltpu.VMEM((n_lon, cols, cap), BF16),
-            pltpu.VMEM((rows * levels, cap), F32),
-            pltpu.VMEM((3, rows * levels, cap), BF16),
-            pltpu.VMEM((3, rows * levels, cols), BF16),
+            pltpu.VMEM((3 * rows * levels, cap), F32),
+            pltpu.VMEM((2 * rows * levels, cap), BF16),
+            pltpu.VMEM((3 * rows * levels, cols), BF16),
             pltpu.VMEM((rows * levels, cols), F32),
             pltpu.VMEM((3, ext, lanes), F32),
             pltpu.VMEM((2, rows, 128), F32),
@@ -348,7 +359,7 @@
         name="analysis",
     )(
         state, coef_lon, coef_lat, land_sea, send_cols, send_count,
-        obs_value.reshape(levels, slots), obs_weight.reshape(levels, slots),
+        obs_value, obs_weight,
     )
     return jnp.transpose(out, (1, 0, 2))
 

time: 36.3 us -> 39.6 us (1.091)
  local copies, waits for them, and re-layouts: 3.12 us -> 7.68 us
  Pallas kernels: 32.6 us -> 31.4 us
    unnamed x13 -> x16, local copies, waits for them, and re-layouts: 2.02 us -> 6.58 us
    pallas_call x1, Pallas kernels: 32.6 us -> 31.4 us  [body(): pl.pallas_call(functools.partial(kernel, n_lon, n_lat), out_shape=jax.Sha...]
where the time goes in v3:
time: 39.6 us; the launch traced here: 39.1 us
  Pallas kernels  31.4 us (79%)
  local copies, waits for them, and re-layouts  7.68 us (19%)
    pallas_call x1, Pallas kernels, body(): pl.pallas_call(functools.partial(kernel, n_lon, n_lat), out_shape=jax.Sha...  31.4 us
    unnamed x16, local copies, waits for them, and re-layouts  6.58 us
    transpose x1, local copies, waits for them, and re-layouts, body(): return jnp.transpose(out, (1, 0, 2))  1.1 us

profile of v3, /device:TPU:0, one launch (start us, length us, event | category | flops | bytes accessed | tf_op | source)
XLA Modules:
  0.0 39.1 jit_solution(6618438487924470046)
XLA Ops:
  0.0 0.0 copy-start
  0.0 1.0 %copy-done = f32[16,32,256]{2,1,0:T(8,128)S(1)} copy-done((f32[16,32,256]{2,1,0:T(8,128)S(1)}, f32[16,32,256]{2,1,0:T(8,128)}, u32[]{:S(2)}) %copy-start) | copy-done | bytes 524312
  1.0 0.0 copy-start.1
  1.0 0.9 %copy-done.1 = f32[16,1,4096]{2,1,0:T(1,128)S(1)} copy-done((f32[16,1,4096]{2,1,0:T(1,128)S(1)}, f32[16,1,4096]{2,1,0:T(1,128)}, u32[]{:S(2)}) %copy-start.1) | copy-done | bytes 262168
  2.0 0.0 copy-start.2
  2.0 0.9 %copy-done.2 = f32[16,1,4096]{2,1,0:T(1,128)S(1)} copy-done((f32[16,1,4096]{2,1,0:T(1,128)S(1)}, f32[16,1,4096]{2,1,0:T(1,128)}, u32[]{:S(2)}) %copy-start.2) | copy-done | bytes 262168
  2.9 0.0 copy-start.3
  2.9 0.8 %copy-done.3 = f32[32,256]{1,0:T(8,128)S(1)} copy-done((f32[32,256]{1,0:T(8,128)S(1)}, f32[32,256]{1,0:T(8,128)}, u32[]{:S(2)}) %copy-start.3) | copy-done | bytes 32792
  3.7 0.0 copy-start.4
  3.7 0.8 %copy-done.4 = f32[32,256]{1,0:T(8,128)S(1)} copy-done((f32[32,256]{1,0:T(8,128)S(1)}, f32[32,256]{1,0:T(8,128)}, u32[]{:S(2)}) %copy-start.4) | copy-done | bytes 32792
  4.5 0.0 copy-start.5
  4.5 0.8 %copy-done.5 = s32[32,256]{1,0:T(8,128)S(1)} copy-done((s32[32,256]{1,0:T(8,128)S(1)}, s32[32,256]{1,0:T(8,128)}, u32[]{:S(2)}) %copy-start.5) | copy-done | bytes 32792
  5.2 0.0 copy-start.6
  5.2 0.7 %copy-done.6 = s32[1,4096]{1,0:T(1,128)S(1)} copy-done((s32[1,4096]{1,0:T(1,128)S(1)}, s32[1,4096]{1,0:T(1,128)}, u32[]{:S(2)}) %copy-start.6) | copy-done | bytes 16408
  5.9 0.0 copy-start.7
  5.9 0.7 %copy-done.7 = s32[1,8]{1,0:T(1,128)S(1)} copy-done((s32[1,8]{1,0:T(1,128)S(1)}, s32[1,8]{1,0:T(1,128)}, u32[]{:S(2)}) %copy-start.7) | copy-done | bytes 56
  6.6 31.4 %analysis.1 = f32[32,16,256]{2,1,0:T(8,128)S(1)} custom-call(f32[16,32,256]{2,1,0:T(8,128)S(1)} %copy-done, f32[32,256]{1,0:T(8,128)S(1)} %copy-done.3, f32[32,256]{1,0:T(8,128)S(1)} %copy-done.4, s32[32,256]{1,0:T(8,128)S(1)} %copy-done.5, s32[1,4096]{1,0:T(1,128)S(1)} %copy-done.6, s32[1,8]{1,0:T(1,128)S(1)} %copy-done.7, f32[16,1,4096]{2,1,0:T(1,128)S(1)} %copy-done.1, ...), custom_call_target="tpu_custom_call" | custom-call | tf_op jit(solution)/shard_map/analysis/pallas_call | solution.py:324
  38.0 1.1 %copy.9 = f32[16,32,256]{2,1,0:T(8,128)} copy(f32[16,32,256]{2,0,1:T(8,128)S(1)} %bitcast.1) | data formatting | bytes 1048576 | tf_op jit(solution)/shard_map/transpose | solution.py:364
Async XLA Ops:
  0.0 1.0 %copy-start = (f32[16,32,256]{2,1,0:T(8,128)S(1)}, f32[16,32,256]{2,1,0:T(8,128)}, u32[]{:S(2)}) copy-start(f32[16,32,256]{2,1,0:T(8,128)} %state_ref.1) | copy-start | bytes 1572868
  1.0 0.9 %copy-start.1 = (f32[16,1,4096]{2,1,0:T(1,128)S(1)}, f32[16,1,4096]{2,1,0:T(1,128)}, u32[]{:S(2)}) copy-start(f32[16,1,4096]{2,1,0:T(1,128)} %value_ref.1) | copy-start | bytes 786436
  2.0 0.9 %copy-start.2 = (f32[16,1,4096]{2,1,0:T(1,128)S(1)}, f32[16,1,4096]{2,1,0:T(1,128)}, u32[]{:S(2)}) copy-start(f32[16,1,4096]{2,1,0:T(1,128)} %weight_ref.1) | copy-start | bytes 786436
  2.9 0.8 %copy-start.3 = (f32[32,256]{1,0:T(8,128)S(1)}, f32[32,256]{1,0:T(8,128)}, u32[]{:S(2)}) copy-start(f32[32,256]{1,0:T(8,128)} %coef_lon_ref.1) | copy-start | bytes 98308
  3.7 0.8 %copy-start.4 = (f32[32,256]{1,0:T(8,128)S(1)}, f32[32,256]{1,0:T(8,128)}, u32[]{:S(2)}) copy-start(f32[32,256]{1,0:T(8,128)} %coef_lat_ref.1) | copy-start | bytes 98308
  4.5 0.8 %copy-start.5 = (s32[32,256]{1,0:T(8,128)S(1)}, s32[32,256]{1,0:T(8,128)}, u32[]{:S(2)}) copy-start(s32[32,256]{1,0:T(8,128)} %land_ref.1) | copy-start | bytes 98308
  5.2 0.7 %copy-start.6 = (s32[1,4096]{1,0:T(1,128)S(1)}, s32[1,4096]{1,0:T(1,128)}, u32[]{:S(2)}) copy-start(s32[1,4096]{1,0:T(1,128)} %cols_ref.1) | copy-start | bytes 49156
  5.9 0.7 %copy-start.7 = (s32[1,8]{1,0:T(1,128)S(1)}, s32[1,8]{1,0:T(1,128)}, u32[]{:S(2)}) copy-start(s32[1,8]{1,0:T(1,128)} %count_ref.1) | copy-start | bytes 100

commit v4 on v3

--- a/solution.py
+++ b/solution.py
@@ -23,18 +23,19 @@
 
 def kernel(
     n_lon, n_lat,
+    state_in, coef_lon_in, coef_lat_in, land_in, cols_in, count_in, value_in, weight_in,
+    out_ref,
     state_ref, coef_lon_ref, coef_lat_ref, land_ref, cols_ref, count_ref, value_ref, weight_ref,
-    out_ref,
-    recv, seen, hot, spread, spread_bf, pieces, scattered, coefs, coef_out, coef_west, coef_east,
+    outgoing,    recv, seen, hot, spread, spread_bf, pieces, scattered, coefs, coef_out, coef_west, coef_east,
     east_b, west_b, north_b, field, edge_out, edge_west, edge_east,
-    own_sem, send_sem, recv_sem, csend_sem, crecv_sem, gsend_sem, grecv_sem,
+    load_sem, send_sem, recv_sem, csend_sem, crecv_sem, gsend_sem, grecv_sem,
 ):
     levels, rows, cols = state_ref.shape
     cells = rows * levels
     halo = PASSES
     ext = rows + 2 * halo
     lanes = cols + 128
-    cap = recv.shape[4]
+    cap = recv.shape[3]
     lon = lax.axis_index("lon")
     lat = lax.axis_index("lat")
     east, west = lax.rem(lon + 1, n_lon), lax.rem(lon + n_lon - 1, n_lon)
@@ -47,6 +48,16 @@
         at(lon, north), at(lon, south), at(east, lat), at(west, lat),
         at(east, north), at(west, north), at(east, south), at(west, south),
     ]
+    loads = [
+        pltpu.make_async_copy(src, dst, load_sem.at[i])
+        for i, (src, dst) in enumerate((
+            (value_in, value_ref), (weight_in, weight_ref), (state_in, state_ref),
+            (coef_lon_in, coef_lon_ref), (coef_lat_in, coef_lat_ref), (land_in, land_ref),
+            (cols_in, cols_ref), (count_in, count_ref),
+        ))
+    ]
+    for load in loads:
+        load.start()
     barrier = pltpu.get_barrier_semaphore()
     for step in range(1, n_lon):
         pl.semaphore_signal(
@@ -55,6 +66,34 @@
     for place in (0, 1, 4, 5, 6, 7):
         pl.semaphore_signal(barrier, inc=1, device_id=around[place], device_id_type=MESH)
 
+    loads[0].wait()
+    loads[1].wait()
+    for peer in range(n_lon):
+        outgoing[peer, 0] = value_ref[:, 0, peer * cap:(peer + 1) * cap]
+        outgoing[peer, 1] = weight_ref[:, 0, peer * cap:(peer + 1) * cap]
+    pl.semaphore_wait(barrier, n_lon - 1 + 6)
+
+    def profile_copy(step):
+        peer = lax.rem(lon + step, n_lon)
+        return pltpu.make_async_remote_copy(
+            src_ref=outgoing.at[peer],
+            dst_ref=recv.at[step],
+            send_sem=send_sem.at[step],
+            recv_sem=recv_sem.at[step],
+            device_id=at(peer, lat),
+            device_id_type=MESH,
+        )
+
+    half = n_lon // 2
+    order = []
+    for off in range(half, 0, -1):
+        order += [off] if 2 * off == n_lon else [off, n_lon - off]
+    for step in order:
+        profile_copy(step).start()
+    recv[0] = outgoing[lon]
+
+    for load in loads[2:]:
+        load.wait()
     here = pl.ds(halo, rows)
     coefs[0, here, 0:cols] = land_ref[...].astype(F32)
     coefs[1, here, 0:cols] = coef_lon_ref[...]
@@ -71,45 +110,6 @@
     coef_out[0] = to_east
     coef_out[1] = to_west
 
-    for r in range(rows):
-        parts = pieces_of(state_ref[:, r, :])
-        for i in range(3):
-            pieces[cells * i + levels * r:cells * i + levels * (r + 1), :] = parts[i]
-
-    pl.semaphore_wait(barrier, n_lon - 1 + 6)
-
-    sources = (value_ref, weight_ref)
-
-    def profile_copy(which, step):
-        peer = lax.rem(lon + step, n_lon)
-        start = pl.multiple_of(peer * cap, 128)
-        return pltpu.make_async_remote_copy(
-            src_ref=sources[which].at[:, :, pl.ds(start, cap)],
-            dst_ref=recv.at[which, step],
-            send_sem=send_sem.at[which, step],
-            recv_sem=recv_sem.at[which, step],
-            device_id=at(peer, lat),
-            device_id_type=MESH,
-        )
-
-    half = n_lon // 2
-    order = []
-    for off in range(half, 0, -1):
-        order += [off] if 2 * off == n_lon else [off, n_lon - off]
-    for step in order:
-        for which in (0, 1):
-            profile_copy(which, step).start()
-    own = [
-        pltpu.make_async_copy(
-            sources[which].at[:, :, pl.ds(pl.multiple_of(lon * cap, 128), cap)],
-            recv.at[which, 0],
-            own_sem.at[which],
-        )
-        for which in (0, 1)
-    ]
-    for copy in own:
-        copy.start()
-
     top, bottom = pl.ds(rows - halo, halo), pl.ds(0, halo)
     low_rim, high_rim = pl.ds(0, halo), pl.ds(halo + rows, halo)
     coef_moves = [
@@ -131,6 +131,11 @@
     ]
     for copy in coef_copies:
         copy.start()
+
+    for r in range(rows):
+        parts = pieces_of(state_ref[:, r, :])
+        for i in range(3):
+            pieces[cells * i + levels * r:cells * i + levels * (r + 1), :] = parts[i]
 
     def places(step):
         holder = lax.rem(lon + n_lon - step, n_lon)
@@ -188,19 +193,14 @@
     def scatter_step(turn, carry):
         step = jnp.where(turn % 2 == 1, (turn + 1) // 2, (n_lon - turn // 2) % n_lon)
         holder, row, _ = places(step)
-        for which in (0, 1):
-
-            @pl.when(step == 0)
-            def _():
-                own[which].wait()
-
-            @pl.when(step != 0)
-            def _():
-                profile_copy(which, step).wait_recv()
+
+        @pl.when(step != 0)
+        def _():
+            profile_copy(step).wait_recv()
 
         slot = lax.broadcasted_iota(jnp.int32, (levels, cap), 1)
         usable = jnp.where(slot < count_ref[0, holder], 1.0, 0.0)
-        weighted = recv[1, step, :, 0, :] * (recv[0, step, :, 0, :] - seen[step]) * usable
+        weighted = recv[step, 1] * (recv[step, 0] - seen[step]) * usable
         parts = pieces_of(weighted)[:2]
         row_b = jnp.broadcast_to(row.astype(F32), (levels, cap)).astype(BF16)
         nothing = jnp.zeros((levels, cap), BF16)
@@ -304,8 +304,7 @@
         advance(t, halo + rows - t, ext - t)
 
     for step in order:
-        for which in (0, 1):
-            profile_copy(which, step).wait_send()
+        profile_copy(step).wait_send()
     for copy in field_copies:
         copy.wait_send()
 
@@ -319,15 +318,23 @@
     ext, lanes = rows + 2 * PASSES, cols + 128
     blocks = rows * PASSES // 128
     vmem = pl.BlockSpec(memory_space=pltpu.VMEM)
-    anywhere = pl.BlockSpec(memory_space=pl.ANY)
     dma = pltpu.SemaphoreType.DMA
     out = pl.pallas_call(
         functools.partial(kernel, n_lon, n_lat),
         out_shape=jax.ShapeDtypeStruct((rows, levels, cols), F32),
-        in_specs=[vmem] * 5 + [pl.BlockSpec(memory_space=pltpu.SMEM)] + [anywhere] * 2,
+        in_specs=[pl.BlockSpec(memory_space=pltpu.HBM)] * 8,
         out_specs=vmem,
         scratch_shapes=[
-            pltpu.VMEM((2, n_lon, levels, 1, cap), F32),
+            pltpu.VMEM((levels, rows, cols), F32),
+            pltpu.VMEM((rows, cols), F32),
+            pltpu.VMEM((rows, cols), F32),
+            pltpu.VMEM((rows, cols), jnp.int32),
+            pltpu.VMEM((1, slots), jnp.int32),
+            pltpu.SMEM((1, n_lon), jnp.int32),
+            pltpu.VMEM((levels, 1, slots), F32),
+            pltpu.VMEM((levels, 1, slots), F32),
+            pltpu.VMEM((n_lon, 2, levels, cap), F32),
+            pltpu.VMEM((n_lon, 2, levels, cap), F32),
             pltpu.VMEM((n_lon, levels, cap), F32),
             pltpu.VMEM((n_lon, cols, cap), BF16),
             pltpu.VMEM((3 * rows * levels, cap), F32),
@@ -345,16 +352,16 @@
             pltpu.VMEM((2, blocks, levels, 128), F32),
             pltpu.VMEM((blocks + 2, levels, 128), F32),
             pltpu.VMEM((blocks + 2, levels, 128), F32),
-            dma((2,)),
-            dma((2, n_lon)),
-            dma((2, n_lon)),
+            dma((8,)),
+            dma((n_lon,)),
+            dma((n_lon,)),
             dma((8,)),
             dma((8,)),
             dma((8,)),
             dma((8,)),
         ],
         compiler_params=pltpu.CompilerParams(
-            collective_id=0, has_side_effects=True, vmem_limit_bytes=48 * 2**20
+            collective_id=0, has_side_effects=True, vmem_limit_bytes=64 * 2**20
         ),
         name="analysis",
     )(

time: 39.6 us -> 33.9 us (0.86)
  local copies, waits for them, and re-layouts: 7.68 us -> 2.14 us
    unnamed x16 -> x0, local copies, waits for them, and re-layouts: 6.58 us -> none
    transpose x1, local copies, waits for them, and re-layouts: 1.1 us -> 2.14 us  [body(): return jnp.transpose(out, (1, 0, 2))]
where the time goes in v4:
time: 33.9 us; the launch traced here: 33.6 us
  Pallas kernels  31.5 us (93%)
  local copies, waits for them, and re-layouts  2.14 us (6%)
    pallas_call x1, Pallas kernels, body(): pl.pallas_call(functools.partial(kernel, n_lon, n_lat), out_shape=jax.Sha...  31.5 us
    transpose x1, local copies, waits for them, and re-layouts, body(): return jnp.transpose(out, (1, 0, 2))  2.14 us

profile of v4, /device:TPU:0, one launch (start us, length us, event | category | flops | bytes accessed | tf_op | source)
XLA Modules:
  0.0 33.6 jit_solution(5090563377925094915)
XLA Ops:
  0.0 31.5 %analysis.1 = f32[32,16,256]{2,1,0:T(8,128)} custom-call(f32[16,32,256]{2,1,0:T(8,128)} %state_in.1, f32[32,256]{1,0:T(8,128)} %coef_lon_in.1, f32[32,256]{1,0:T(8,128)} %coef_lat_in.1, s32[32,256]{1,0:T(8,128)} %land_in.1, s32[1,4096]{1,0:T(1,128)} %cols_in.1, s32[1,8]{1,0:T(1,128)} %count_in.1, f32[16,1,4096]{2,1,0:T(1,128)} %value_in.1, ...), custom_call_target="tpu_custom_call" | custom-call | tf_op jit(solution)/shard_map/analysis/pallas_call | solution.py:322
  31.5 2.1 %copy.9 = f32[16,32,256]{2,1,0:T(8,128)} copy(f32[16,32,256]{2,0,1:T(8,128)} %bitcast.1) | data formatting | bytes 1048576 | tf_op jit(solution)/shard_map/transpose | solution.py:371

commit v5 on v4

--- a/solution.py
+++ b/solution.py
@@ -71,28 +71,7 @@
     for peer in range(n_lon):
         outgoing[peer, 0] = value_ref[:, 0, peer * cap:(peer + 1) * cap]
         outgoing[peer, 1] = weight_ref[:, 0, peer * cap:(peer + 1) * cap]
-    pl.semaphore_wait(barrier, n_lon - 1 + 6)
-
-    def profile_copy(step):
-        peer = lax.rem(lon + step, n_lon)
-        return pltpu.make_async_remote_copy(
-            src_ref=outgoing.at[peer],
-            dst_ref=recv.at[step],
-            send_sem=send_sem.at[step],
-            recv_sem=recv_sem.at[step],
-            device_id=at(peer, lat),
-            device_id_type=MESH,
-        )
-
-    half = n_lon // 2
-    order = []
-    for off in range(half, 0, -1):
-        order += [off] if 2 * off == n_lon else [off, n_lon - off]
-    for step in order:
-        profile_copy(step).start()
-    recv[0] = outgoing[lon]
-
-    for load in loads[2:]:
+    for load in loads[3:6]:
         load.wait()
     here = pl.ds(halo, rows)
     coefs[0, here, 0:cols] = land_ref[...].astype(F32)
@@ -129,9 +108,31 @@
         )
         for i, (src, dst) in enumerate(coef_moves)
     ]
+    pl.semaphore_wait(barrier, n_lon - 1 + 6)
     for copy in coef_copies:
         copy.start()
 
+    def profile_copy(step):
+        peer = lax.rem(lon + step, n_lon)
+        return pltpu.make_async_remote_copy(
+            src_ref=outgoing.at[peer],
+            dst_ref=recv.at[step],
+            send_sem=send_sem.at[step],
+            recv_sem=recv_sem.at[step],
+            device_id=at(peer, lat),
+            device_id_type=MESH,
+        )
+
+    half = n_lon // 2
+    order = []
+    for off in range(half, 0, -1):
+        order += [off] if 2 * off == n_lon else [off, n_lon - off]
+    for step in order:
+        profile_copy(step).start()
+    recv[0] = outgoing[lon]
+
+    for load in (loads[2], loads[6], loads[7]):
+        load.wait()
     for r in range(rows):
         parts = pieces_of(state_ref[:, r, :])
         for i in range(3):
@@ -191,7 +192,8 @@
     scattered[...] = jnp.zeros_like(scattered)
 
     def scatter_step(turn, carry):
-        step = jnp.where(turn % 2 == 1, (turn + 1) // 2, (n_lon - turn // 2) % n_lon)
+        off = half - turn // 2
+        step = jnp.where(turn == 0, 0, jnp.where(turn % 2 == 1, n_lon - off, off))
         holder, row, _ = places(step)
 
         @pl.when(step != 0)
@@ -285,7 +287,7 @@
             flux_west = twice(west_b[e]) * (g - pltpu.roll(g, 1, axis=1))
             new = g + flux_east - flux_west + flux_north - flux_south
             if t == PASSES:
-                out_ref[e - halo] = new[:, 0:cols]
+                out_ref[:, e - halo, :] = new[:, 0:cols]
             else:
                 field[t, e] = new
             g, flux_south = g_north, flux_north
@@ -319,9 +321,9 @@
     blocks = rows * PASSES // 128
     vmem = pl.BlockSpec(memory_space=pltpu.VMEM)
     dma = pltpu.SemaphoreType.DMA
-    out = pl.pallas_call(
+    return pl.pallas_call(
         functools.partial(kernel, n_lon, n_lat),
-        out_shape=jax.ShapeDtypeStruct((rows, levels, cols), F32),
+        out_shape=jax.ShapeDtypeStruct((levels, rows, cols), F32),
         in_specs=[pl.BlockSpec(memory_space=pltpu.HBM)] * 8,
         out_specs=vmem,
         scratch_shapes=[
@@ -368,7 +370,6 @@
         state, coef_lon, coef_lat, land_sea, send_cols, send_count,
         obs_value, obs_weight,
     )
-    return jnp.transpose(out, (1, 0, 2))
 
 
 def solution(mesh):

time: 33.9 us -> 32.9 us (0.971)
  Pallas kernels: 31.5 us -> 30.8 us
    transpose x1 -> x0, local copies, waits for them, and re-layouts: 2.14 us -> none  [body(): return jnp.transpose(out, (1, 0, 2))]
    unnamed x0 -> x1, local copies, waits for them, and re-layouts: none -> 1.88 us
    pallas_call x1, Pallas kernels: 31.5 us -> 30.8 us  [body(): pl.pallas_call(functools.partial(kernel, n_lon, n_lat), out_shape=jax.Sha...]
where the time goes in v5:
time: 32.9 us; the launch traced here: 32.7 us
  Pallas kernels  30.8 us (94%)
  local copies, waits for them, and re-layouts  1.88 us (6%)
    pallas_call x1, Pallas kernels, body(): pl.pallas_call(functools.partial(kernel, n_lon, n_lat), out_shape=jax.Sha...  30.8 us
    unnamed x1, local copies, waits for them, and re-layouts  1.88 us

profile of v5, /device:TPU:0, one launch (start us, length us, event | category | flops | bytes accessed | tf_op | source)
XLA Modules:
  0.0 32.7 jit_solution(9529219898003737594)
XLA Ops:
  0.0 30.8 %analysis.1 = f32[16,32,256]{2,1,0:T(8,128)} custom-call(f32[16,32,256]{2,1,0:T(8,128)} %state_in.1, f32[32,256]{1,0:T(8,128)} %coef_lon_in.1, f32[32,256]{1,0:T(8,128)} %coef_lat_in.1, s32[32,256]{1,0:T(8,128)} %land_in.1, s32[1,4096]{1,0:T(1,128)} %cols_in.1, s32[1,8]{1,0:T(1,128)} %count_in.1, f32[16,1,4096]{2,1,0:T(1,128)} %value_in.1, ...), custom_call_target="tpu_custom_call" | custom-call | tf_op jit(solution)/shard_map/analysis/pallas_call | solution.py:324
  30.8 1.9 %copy.10 = f32[16,32,256]{2,1,0:T(8,128)} copy(f32[16,32,256]{2,1,0:T(8,128)} %analysis.1) | data formatting | bytes 1048576
